TPU v7x, 32 devices: a whole 2x2x4 slice. The times are simulated.
32 devices in a mesh: groups: 2 (over x), band: 16 (over z, y, core).
Axes of the slice: x: 2, y: 2, z: 4, core: 2. Of those that a mesh axis runs over, the one named last changes fastest.
Arguments:
- nest_tokens: bfloat16 [16384, 256], P(('groups', 'band')), parts along dimension 0
- global_tokens: bfloat16 [4096, 256], P(('groups', 'band')), parts along dimension 0
- block_ids: int32 [128, 4], P(('groups', 'band')), parts along dimension 0, may hold values from 0 to 15, as said below
- list_length: int32 [128], P(('groups', 'band')), parts along dimension 0, may hold values from 2 to 4, as said below
- w_query: bfloat16 [256, 256], replicated, may hold values from -0.375 to 0.375
- w_keyval: bfloat16 [256, 512], replicated, may hold values from -0.375 to 0.375
- w_out: bfloat16 [256, 256], replicated, may hold values from -0.375 to 0.375
- d_output: bfloat16 [16384, 256], P(('groups', 'band')), parts along dimension 0, may hold values from -6 to 6
Outputs:
- output: bfloat16 [16384, 256], P(('groups', 'band')), parts along dimension 0
- d_nest: bfloat16 [16384, 256], P(('groups', 'band')), parts along dimension 0
- d_global: bfloat16 [4096, 256], P(('groups', 'band')), parts along dimension 0
- grad_query: float32 [512, 256], P('groups'), parts along dimension 0
- grad_keyval: float32 [512, 512], P('groups'), parts along dimension 0
- grad_out: float32 [512, 256], P('groups'), parts along dimension 0
There are 2 independent parts, one for each index of `groups`. A program takes and returns all parts, laid end to end along the dimension named above; an argument that names none is the same for every part. Nothing has to cross between parts.
Inputs may be any that keep to these rules, and one draw needn't show every extreme that they name: `block_ids`: each row holds 4 different global block numbers, all owned by the aligned group of 16 devices of band that holds the nest block; the global blocks of device d are d*1 to (d+1) - 1. Only the first list_length[b] entries of row b are used.
All inputs are finite; a program needn't handle non-finite values.
Results may differ from a plain program's by a relative error of at most 0.0095.
The roundings to bfloat16 on the way count: a program that leaves them out, or rounds other values in their place, can miss the bound.
Values may be sent and summed in bfloat16 or wider, within the bound.
A program may use at most 128 MiB of HBM per device.

v0:
```python
import math

import jax
import jax.numpy as jnp
from jax import lax
from jax.sharding import PartitionSpec as P

HD = 32
BT = 128
GB = 128
LIST = 4
SUB = 16


def from_partner(block, axis, apart):
    count = lax.axis_size(axis)
    route = []
    for low in range(count):
        high = low | 1 << apart
        if high != low and high < count:
            route += [(low, high), (high, low)]
    return lax.ppermute(block, axis, route)


def attend_block(query_block, footprint, live_count, grad_block):
    features = query_block.shape[1]
    heads = features // HD
    slots = footprint.shape[0] * footprint.shape[1]
    flat = footprint.reshape(slots, 2 * features)
    keys = flat[:, :features].reshape(slots, heads, HD)
    values = flat[:, features:].reshape(slots, heads, HD)
    queries = query_block.reshape(-1, heads, HD)
    slot_block = jnp.arange(slots, dtype=jnp.int32) // footprint.shape[1]
    live_slots = slot_block < live_count
    score_scale = HD ** (-0.5)
    scores = (
        jnp.einsum("qhd,khd->hqk", queries, keys, preferred_element_type=jnp.float32) * score_scale
    )
    scores = jnp.where(live_slots[None, None, :], scores, -jnp.inf)
    top_score = jnp.max(scores, axis=-1, keepdims=True)
    raw_weights = jnp.exp(scores - top_score)
    probs = raw_weights / jnp.sum(raw_weights, axis=-1, keepdims=True)
    probs_low = probs.astype(jnp.bfloat16)
    attended = jnp.einsum("hqk,khd->qhd", probs_low, values, preferred_element_type=jnp.float32)
    attended = attended.astype(jnp.bfloat16).reshape(-1, features)
    grads = grad_block.reshape(-1, heads, HD)
    d_probs = jnp.einsum("qhd,khd->hqk", grads, values, preferred_element_type=jnp.float32)
    centre = jnp.sum(probs * d_probs, axis=-1, keepdims=True)
    d_scores = (probs * (d_probs - centre) * score_scale).astype(jnp.bfloat16)
    d_queries = jnp.einsum("hqk,khd->qhd", d_scores, keys, preferred_element_type=jnp.float32)
    d_queries = d_queries.astype(jnp.bfloat16).reshape(-1, features)
    d_keys = jnp.einsum(
        "hqk,qhd->khd", d_scores, queries, preferred_element_type=jnp.float32
    ).reshape(slots, features)
    d_values = jnp.einsum(
        "hqk,qhd->khd", probs_low, grads, preferred_element_type=jnp.float32
    ).reshape(slots, features)
    d_foot = jnp.concatenate([d_keys, d_values], axis=-1).reshape(
        footprint.shape[0], footprint.shape[1], 2 * features
    )
    return (attended, d_queries, d_foot)


def shards(nest_tokens, global_tokens, block_ids, list_length, w_query, w_keyval, w_out, d_output):
    features = nest_tokens.shape[1]
    sections = SUB.bit_length() - 1
    device_index = lax.axis_index("band")
    position = device_index % SUB
    own_rows = global_tokens.shape[0]
    region_first = (device_index - position) * (own_rows // GB)
    region = jnp.dot(global_tokens, w_keyval, preferred_element_type=jnp.float32).astype(
        jnp.bfloat16
    )
    for section_bit in range(sections):
        partner = from_partner(region, "band", section_bit)
        upper_side = position // (1 << section_bit) % 2
        region = jnp.where(
            upper_side == 1,
            jnp.concatenate([partner, region], axis=0),
            jnp.concatenate([region, partner], axis=0),
        )
    region_blocks = region.reshape(-1, GB, 2 * features)
    queries = jnp.dot(nest_tokens, w_query, preferred_element_type=jnp.float32).astype(jnp.bfloat16)
    grad_attn = jnp.dot(d_output, w_out.T, preferred_element_type=jnp.float32).astype(jnp.bfloat16)
    local_ids = block_ids - region_first
    group_size = 4
    nest_blocks = nest_tokens.shape[0] // BT
    rounds = nest_blocks // group_size

    def one_block(query_block, row_ids, live_count, grad_block):
        return attend_block(query_block, region_blocks[row_ids], live_count, grad_block)

    def visit(carry, inputs):
        query_group, id_group, count_group, grad_group = inputs
        attended, d_queries, d_foot = jax.vmap(one_block)(
            query_group, id_group, count_group, grad_group
        )
        carry = carry.at[id_group.reshape(-1)].add(d_foot.reshape(-1, GB, 2 * features))
        return (carry, (attended, d_queries))

    start_pairs = jnp.zeros(region_blocks.shape, jnp.float32)
    d_region, (attended, d_queries) = lax.scan(
        visit,
        start_pairs,
        (
            queries.reshape(rounds, group_size, BT, features),
            local_ids.reshape(rounds, group_size, LIST),
            list_length.reshape(rounds, group_size),
            grad_attn.reshape(rounds, group_size, BT, features),
        ),
    )
    attended = attended.reshape(-1, features)
    d_queries = d_queries.reshape(-1, features)
    d_region = d_region.reshape(-1, 2 * features)
    output = jnp.dot(attended, w_out, preferred_element_type=jnp.float32).astype(jnp.bfloat16)
    d_nest = jnp.dot(d_queries, w_query.T, preferred_element_type=jnp.float32).astype(jnp.bfloat16)
    weights_wide = w_keyval.astype(jnp.float32)
    buffer = d_region.reshape(SUB, own_rows, 2 * features)
    for section_bit in reversed(range(sections)):
        halfway = buffer.shape[0] // 2
        upper_side = position // (1 << section_bit) % 2
        kept_half = jnp.where(upper_side == 1, buffer[halfway:], buffer[:halfway])
        sent_half = jnp.where(upper_side == 1, buffer[:halfway], buffer[halfway:])
        buffer = kept_half + from_partner(
            sent_half.astype(jnp.bfloat16), "band", section_bit
        ).astype(sent_half.dtype)
    own_pairs = buffer.reshape(own_rows, 2 * features)
    d_global = jnp.dot(own_pairs, weights_wide.T, precision=lax.Precision.HIGHEST).astype(
        jnp.bfloat16
    )
    keyval_term = jnp.dot(
        global_tokens.astype(jnp.float32).T, own_pairs, precision=lax.Precision.HIGHEST
    )
    query_term = jnp.dot(nest_tokens.T, d_queries, preferred_element_type=jnp.float32)
    out_term = jnp.dot(attended.T, d_output, preferred_element_type=jnp.float32)
    query_sum, keyval_sum, out_sum = lax.psum((query_term, keyval_term, out_term), "band")
    norm_factor = 1.0 / math.sqrt(nest_tokens.shape[0] * lax.axis_size("band"))
    return (
        output,
        d_nest,
        d_global,
        query_sum * norm_factor,
        keyval_sum * norm_factor,
        out_sum * norm_factor,
    )


def solution(mesh):
    in_specs = (
        P(("groups", "band"), None),
        P(("groups", "band"), None),
        P(("groups", "band"), None),
        P(("groups", "band")),
        P(),
        P(),
        P(),
        P(("groups", "band"), None),
    )
    out_specs = (
        P(("groups", "band"), None),
        P(("groups", "band"), None),
        P(("groups", "band"), None),
        P("groups", None),
        P("groups", None),
        P("groups", None),
    )
    return jax.shard_map(shards, mesh=mesh, in_specs=in_specs, out_specs=out_specs, check_vma=False)
```

profile of v0, /device:TPU:0, one launch (start us, length us, event | category | flops | bytes accessed | tf_op | source)
XLA Modules:
  0.0 375.3 jit_solution(784465061122481372)
XLA Ops:
  7.3 1.3 convolution_convert_fusion.4
  9.1 1.0 collective-permute-done
  10.1 2.9 collective-permute-start.1
  13.0 6.6 %collective-permute-done.1 = bf16[256,512]{1,0:T(8,128)(2,1)S(1)} collective-permute-done((bf16[256,512]{1,0:T(8,128)(2,1)S(1)}, bf16[256,512]{1,0:T(8,128)(2,1)S(1)}, u32[]{:S(2)}, u32[]{:S(2)}) %collective-permute-start.1) | collective-permute-done | bytes 262176 | tf_op jit(solution)/shard_map/ppermute | solution.py:22
  19.9 1.9 collective-permute-start.2
  21.7 0.7 compare_select_fusion
  22.5 10.9 %collective-permute-done.2 = bf16[512,512]{1,0:T(8,128)(2,1)S(1)} collective-permute-done((bf16[512,512]{1,0:T(8,128)(2,1)S(1)}, bf16[512,512]{1,0:T(8,128)(2,1)S(1)}, u32[]{:S(2)}, u32[]{:S(2)}) %collective-permute-start.2) | collective-permute-done | bytes 524320 | tf_op jit(solution)/shard_map/ppermute | solution.py:22
  33.9 2.6 collective-permute-start.3
  36.8 0.8 reshape.150
  38.0 0.8 reshape.153
  38.9 42.2 %collective-permute-done.3 = bf16[1024,512]{1,0:T(8,128)(2,1)S(1)} collective-permute-done((bf16[1024,512]{1,0:T(8,128)(2,1)S(1)}, bf16[1024,512]{1,0:T(8,128)(2,1)S(1)}, u32[]{:S(2)}, u32[]{:S(2)}) %collective-permute-start.3) | collective-permute-done | bytes 1048608 | tf_op jit(solution)/shard_map/ppermute | solution.py:22
  81.1 1.9 maximum_select_fusion
  83.0 2.3 gather_fusion
  85.3 1.1 fusion.64
  87.0 1.9 copy.59
  88.9 1.3 fusion.52
  90.2 2.9 fusion.65
  93.1 5.0 %fusion.49 = f32[4,8,128,512]{3,2,1,0:T(8,128)} fusion(bf16[4,512,8,32]{1,3,2,0:T(8,128)(2,1)S(1)} %bitcast.69, bf16[4,128,8,32]{1,0,3,2:T(4,128)(2,1)S(1)} %copy-done.4), kind=kOutput, calls=%fused_computation.60 | convolution fusion | flops 134217728 | bytes 9699328 | tf_op jit(solution)/shard_map/while/body/eval_jaxpr/vmap(qhd,khd->hqk)/dot_general | solution.py:47
  98.1 0.7 copy-done.13
  99.0 1.5 fusion.19
  100.4 1.4 copy.51
  101.8 1.9 concatenate.42
  103.7 34.5 %fusion.22 = f32[4,512,8,32]{1,3,2,0:T(8,128)} fusion(f32[4,8,128,512]{3,2,1,0:T(8,128)} %fusion.49, bf16[4,128,8,32]{1,0,3,2:T(4,128)(2,1)} %reshape.150, f32[4,8,128,512]{3,2,1,0:T(8,128)} %copy-done.13, f32[4,8,128]{2,1,0:T(8,128)} %copy-done.14), kind=kOutput, calls=%fused_computation.25 | convolution fusion | flops 148902400 | bytes 19152896 | tf_op jit(solution)/shard_map/while/body/eval_jaxpr/vmap(hqk,qhd->khd)/dot_general | solution.py:52
  138.2 2.9 copy.49
  141.2 1.9 concatenate.41
  143.1 4.4 %pad_maximum_fusion = f32[16,128,512]{1,0,2:T(8,128)} fusion(f32[16,128,256]{1,0,2:T(8,128)} %concatenate.42, f32[16,128,256]{1,0,2:T(8,128)} %concatenate.41), kind=kLoop, calls=%fused_computation.10 | loop fusion | flops 1048576 | bytes 8388608 | tf_op jit(solution)/shard_map/while/body/eval_jaxpr/vmap()/concatenate | solution.py:58
  147.5 5.3 %copy.52 = f32[16,128,512]{2,1,0:T(8,128)} copy(f32[16,128,512]{1,0,2:T(8,128)} %pad_maximum_fusion) | data formatting | bytes 8388608 | tf_op jit(solution)/shard_map/while/body/eval_jaxpr/vmap()/concatenate | solution.py:58
  152.8 2.5 broadcast_in_dim.45
  155.3 9.9 %scatter_fusion = f32[16,128,512]{2,1,0:T(8,128)} fusion(f32[16,128,512]{2,1,0:T(8,128)} %broadcast_in_dim.45, s32[16]{0:T(128)S(1)} %fusion.57, f32[16,128,512]{2,1,0:T(8,128)} %copy.52), kind=kCustom, calls=%fused_computation.1 | custom fusion | flops 1048576 | bytes 12582976 | tf_op jit(solution)/shard_map/while/body/eval_jaxpr/scatter-add | solution.py:98
  165.2 2.4 select_convert_fusion
  167.7 47.6 %collective-permute-done.4 = bf16[8,128,512]{2,1,0:T(8,128)(2,1)S(1)} collective-permute-done((bf16[8,128,512]{2,1,0:T(8,128)(2,1)S(1)}, bf16[8,128,512]{2,1,0:T(8,128)(2,1)S(1)}, u32[]{:S(2)}, u32[]{:S(2)}) %collective-permute-start.4) | collective-permute-done | bytes 1048608 | tf_op jit(solution)/shard_map/ppermute | solution.py:22
  215.3 2.9 convert_add_fusion
  218.4 5.0 %fusion.34 = bf16[4,128,8,32]{1,3,2,0:T(8,128)(2,1)S(1)} fusion(bf16[4,512,8,32]{1,3,2,0:T(8,128)(2,1)S(1)} %bitcast.70, f32[4,8,128,512]{3,2,1,0:T(8,128)} %copy-done.13, f32[4,8,128]{2,1,0:T(8,128)S(1)} %copy-done.15), kind=kOutput, calls=%fused_computation.35 | convolution fusion | flops 138543104 | bytes 9715712 | tf_op jit(solution)/shard_map/while/body/eval_jaxpr/vmap(hqk,khd->qhd)/dot_general | solution.py:44
  223.4 7.8 %collective-permute-done.5 = bf16[4,128,512]{2,1,0:T(8,128)(2,1)S(1)} collective-permute-done((bf16[4,128,512]{2,1,0:T(8,128)(2,1)S(1)}, bf16[4,128,512]{2,1,0:T(8,128)(2,1)S(1)}, u32[]{:S(2)}, u32[]{:S(2)}) %collective-permute-start.5) | collective-permute-done | bytes 524320 | tf_op jit(solution)/shard_map/ppermute | solution.py:22
  231.7 33.3 %fusion.31 = bf16[4,128,8,32]{1,3,2,0:T(8,128)(2,1)S(1)} fusion(bf16[4,512,8,32]{1,3,2,0:T(8,128)(2,1)S(1)} %bitcast.68, f32[4,8,128,512]{3,2,1,0:T(8,128)} %fusion.49, f32[4,8,128,512]{3,2,1,0:T(8,128)} %copy-done.13, f32[4,8,128]{2,1,0:T(8,128)S(1)} %copy-done.15), kind=kOutput, calls=%fused_computation.34 | convolution fusion | flops 149033472 | bytes 18104320 | tf_op jit(solution)/shard_map/while/body/eval_jaxpr/vmap(hqk,khd->qhd)/dot_general | solution.py:50
  265.4 0.9 convolution_bitcast_fusion.1
  266.4 1.1 convert_add_fusion.2
  267.6 1.0 fusion.39
  268.9 1.2 convolution_bitcast_fusion
  270.1 1.0 convolution_convert_fusion.2
  271.1 1.0 convolution_convert_fusion
  272.1 1.0 convolution_convert_fusion.5
  273.1 90.5 %all-reduce.3.cloned.1.call-done = (f32[256,256]{0,1:T(8,128)}, f32[256,512]{0,1:T(8,128)}, f32[256,256]{0,1:T(8,128)}) async-done(((f32[256,256]{0,1:T(8,128)}, f32[256,512]{0,1:T(8,128)}, f32[256,256]{0,1:T(8,128)}), (f32[256,256]{0,1:T(8,128)}, f32[256,512]{0,1:T(8,128)}, f32[256,256]{0,1:T(8,128)})) %all-reduce.3.cloned.1.call-update) | async-done | bytes 1048592 | tf_op jit(solution)/shard_map/psum | solution.py:136
  363.6 1.1 broadcast_multiply_fusion.1
  364.7 0.8 copy.54
  365.5 1.1 broadcast_multiply_fusion
  366.6 1.0 copy.55
  367.6 0.8 copy.56
  (60 shorter events, 4.6 us)
Async XLA Ops:
  7.2 29.3 %copy-start = (bf16[512,256]{1,0:T(8,128)(2,1)S(1)}, bf16[512,256]{1,0:T(8,128)(2,1)}, u32[]{:S(2)}) copy-start(bf16[512,256]{1,0:T(8,128)(2,1)} %param.8) | copy-start | bytes 786436
  7.2 29.3 %copy-start.8 = (bf16[256,256]{1,0:T(8,128)(2,1)S(1)}, bf16[256,256]{1,0:T(8,128)(2,1)}, u32[]{:S(2)}) copy-start(bf16[256,256]{1,0:T(8,128)(2,1)} %param.12) | copy-start | bytes 393220
  7.2 30.4 %copy-start.10 = (bf16[256,256]{1,0:T(8,128)(2,1)S(1)}, bf16[256,256]{1,0:T(8,128)(2,1)}, u32[]{:S(2)}) copy-start(bf16[256,256]{1,0:T(8,128)(2,1)} %param.14) | copy-start | bytes 393220
  7.2 30.4 %copy-start.5 = (bf16[512,256]{1,0:T(8,128)(2,1)S(1)}, bf16[512,256]{1,0:T(8,128)(2,1)}, u32[]{:S(2)}) copy-start(bf16[512,256]{1,0:T(8,128)(2,1)} %param.15) | copy-start | bytes 786436
  7.2 31.6 %copy-start.12 = (s32[4]{0:T(128)S(1)}, s32[4]{0:T(128)}, u32[]{:S(2)}) copy-start(s32[4]{0:T(128)} %param.11) | copy-start | bytes 52
  7.2 356.4 %all-reduce.3.cloned.1.call-start = ((), (), s32[]{:S(2)}) async-start(), calls=%async_computation | async-start | bytes 2097152 | tf_op jit(solution)/shard_map/psum | solution.py:136
  8.5 1.5 collective-permute-start
  10.1 9.6 %collective-permute-start.1 = (bf16[256,512]{1,0:T(8,128)(2,1)S(1)}, bf16[256,512]{1,0:T(8,128)(2,1)S(1)}, u32[]{:S(2)}, u32[]{:S(2)}) collective-permute-start(bf16[256,512]{1,0:T(8,128)(2,1)S(1)} %maximum_select_fusion.3), channel_id=1, source_target_pairs={{0,2},{2,0},{1,3},{3,1},{4,6},{6,4},{5,7},{7,5},{8,10},{10,8},{9,1... | collective-permute-start | bytes 786440 | tf_op jit(solution)/shard_map/ppermute | solution.py:22
  19.9 13.5 %collective-permute-start.2 = (bf16[512,512]{1,0:T(8,128)(2,1)S(1)}, bf16[512,512]{1,0:T(8,128)(2,1)S(1)}, u32[]{:S(2)}, u32[]{:S(2)}) collective-permute-start(bf16[512,512]{1,0:T(8,128)(2,1)S(1)} %maximum_select_fusion.2), channel_id=1, source_target_pairs={{0,4},{4,0},{1,5},{5,1},{2,6},{6,2},{3,7},{7,3},{8,12},{12,8},{9,1... | collective-permute-start | bytes 1572872 | tf_op jit(solution)/shard_map/ppermute | solution.py:22
  33.9 47.2 %collective-permute-start.3 = (bf16[1024,512]{1,0:T(8,128)(2,1)S(1)}, bf16[1024,512]{1,0:T(8,128)(2,1)S(1)}, u32[]{:S(2)}, u32[]{:S(2)}) collective-permute-start(bf16[1024,512]{1,0:T(8,128)(2,1)S(1)} %maximum_select_fusion.1), channel_id=1, source_target_pairs={{0,8},{8,0},{1,9},{9,1},{2,10},{10,2},{3,11},{11,3},{4,12},{12,4},... | collective-permute-start | bytes 3145736 | tf_op jit(solution)/shard_map/ppermute | solution.py:22
  86.4 2.4 copy-start.3
  87.0 6.1 %copy-start.1 = (bf16[4,512,256]{1,2,0:T(8,128)(2,1)}, bf16[4,512,256]{1,2,0:T(8,128)(2,1)S(1)}, u32[]{:S(2)}) copy-start(bf16[4,512,256]{1,2,0:T(8,128)(2,1)S(1)} %copy.58) | copy-start | bytes 3145732
  90.2 3.0 copy-start.4
  93.1 5.7 %copy-start.13 = (f32[4,8,128,512]{3,2,1,0:T(8,128)}, f32[4,8,128,512]{3,2,1,0:T(8,128)S(1)}, u32[]{:S(2)}) copy-start(f32[4,8,128,512]{3,2,1,0:T(8,128)S(1)} %get-tuple-element.59) | copy-start | bytes 25165828
  93.1 5.9 %copy-start.14 = (f32[4,8,128]{2,1,0:T(8,128)}, f32[4,8,128]{2,1,0:T(8,128)S(1)}, u32[]{:S(2)}) copy-start(f32[4,8,128]{2,1,0:T(8,128)S(1)} %get-tuple-element.58) | copy-start | bytes 49156
  167.6 50.7 %copy-start.2 = (bf16[4,512,256]{1,2,0:T(8,128)(2,1)S(1)}, bf16[4,512,256]{1,2,0:T(8,128)(2,1)}, u32[]{:S(2)}) copy-start(bf16[4,512,256]{1,2,0:T(8,128)(2,1)} %copy-done.1) | copy-start | bytes 3145732
  167.6 50.7 %copy-start.15 = (f32[4,8,128]{2,1,0:T(8,128)S(1)}, f32[4,8,128]{2,1,0:T(8,128)}, u32[]{:S(2)}) copy-start(f32[4,8,128]{2,1,0:T(8,128)} %copy-done.14) | copy-start | bytes 49156
  167.6 47.7 %collective-permute-start.4 = (bf16[8,128,512]{2,1,0:T(8,128)(2,1)S(1)}, bf16[8,128,512]{2,1,0:T(8,128)(2,1)S(1)}, u32[]{:S(2)}, u32[]{:S(2)}) collective-permute-start(bf16[8,128,512]{2,1,0:T(8,128)(2,1)S(1)} %select_convert_fusion), channel_id=1, source_target_pairs={{0,8},{8,0},{1,9},{9,1},{2,10},{10,2},{3,11},{11,3},{4,12},{12,4},... | collective-permute-start | bytes 3145736 | tf_op jit(solution)/shard_map/ppermute | solution.py:22
  218.3 12.9 %collective-permute-start.5 = (bf16[4,128,512]{2,1,0:T(8,128)(2,1)S(1)}, bf16[4,128,512]{2,1,0:T(8,128)(2,1)S(1)}, u32[]{:S(2)}, u32[]{:S(2)}) collective-permute-start(bf16[4,128,512]{2,1,0:T(8,128)(2,1)S(1)} %select_convert_fusion.1), channel_id=1, source_target_pairs={{0,4},{4,0},{1,5},{5,1},{2,6},{6,2},{3,7},{7,3},{8,12},{12,8},{9,1... | collective-permute-start | bytes 1572872 | tf_op jit(solution)/shard_map/ppermute | solution.py:22
  231.6 34.8 %collective-permute-start.6 = (bf16[2,128,512]{2,1,0:T(8,128)(2,1)S(1)}, bf16[2,128,512]{2,1,0:T(8,128)(2,1)}, u32[]{:S(2)}, u32[]{:S(2)}) collective-permute-start(bf16[2,128,512]{2,1,0:T(8,128)(2,1)S(1)} %select_convert_fusion.2), channel_id=1, source_target_pairs={{0,2},{2,0},{1,3},{3,1},{4,6},{6,4},{5,7},{7,5},{8,10},{10,8},{9,1... | collective-permute-start | bytes 786440 | tf_op jit(solution)/shard_map/ppermute | solution.py:22
  264.9 2.6 copy-start.6
  264.9 3.9 %copy-start.9 = (bf16[128,256]{1,0:T(8,128)(2,1)S(1)}, bf16[128,256]{1,0:T(8,128)(2,1)}, u32[]{:S(2)}) copy-start(bf16[128,256]{1,0:T(8,128)(2,1)} %param.9) | copy-start | bytes 196612
  265.0 5.2 %copy-start.11 = (bf16[256,256]{1,0:T(8,128)(2,1)S(1)}, bf16[256,256]{1,0:T(8,128)(2,1)}, u32[]{:S(2)}) copy-start(bf16[256,256]{1,0:T(8,128)(2,1)} %param.14) | copy-start | bytes 393220
  265.0 7.1 %copy-start.7 = (bf16[256,512]{1,0:T(8,128)(2,1)S(1)}, bf16[256,512]{1,0:T(8,128)(2,1)}, u32[]{:S(2)}) copy-start(bf16[256,512]{1,0:T(8,128)(2,1)} %param.13) | copy-start | bytes 786436
  267.5 1.4 collective-permute-start.7
Sparse Core Ops, SparseCore 0:
  270.2 93.3 all-reduce.2
where the time goes:
time: 376 us; the launch traced here: 375 us
  waiting for transfers between devices  207 us (55%)
  matrix products  88.4 us (24%)
  other arithmetic  29.7 us (8%)
  local copies, waits for them, and re-layouts  27.7 us (7%)
  between operations  14.4 us (4%)
  starting transfers between devices  8.2 us (2%)
    ppermute x8, waiting for transfers between devices, from_partner(): return lax.ppermute(block, axis, route)  116 us
    psum x1, waiting for transfers between devices, shards(): lax.psum((query_term, keyval_term, out_term), 'band')  90.5 us
    dot_general x1, matrix products, attend_block(): jnp.einsum('hqk,qhd->khd', d_scores, queries, preferred_element_type=jnp....  34.5 us
    dot_general x1, matrix products, attend_block(): jnp.einsum('hqk,khd->qhd', d_scores, keys, preferred_element_type=jnp.flo...  33.3 us
    scatter-add x1, other arithmetic, visit(): carry.at[id_group.reshape(-1)].add(d_foot.reshape(-1, GB, 2 * features))  9.93 us
    concatenate x3, local copies, waits for them, and re-layouts, attend_block(): jnp.concatenate([d_keys, d_values], axis=-1)  9.07 us
    ppermute x8, starting transfers between devices, from_partner(): return lax.ppermute(block, axis, route)  8.16 us
  transfers between devices with their start and end apart: 9, of which 8 were waited for; matrix products, arithmetic and copies ran while one was open for 12% of the time, Pallas kernels for 0%

commit v1 on v0

v1 whole, which is shorter than its diff:
```python
import functools
import math

import jax
import jax.numpy as jnp
from jax import lax
from jax.experimental import pallas as pl
from jax.experimental.pallas import tpu as pltpu
from jax.sharding import PartitionSpec as P

HD = 32
BT = 128
GB = 128
LIST = 4
SUB = 16
F32 = jnp.float32
BF16 = jnp.bfloat16
VMEM_LIMIT = 56 * 1024 * 1024


def mm(a, b, ca=1, cb=0):
    return lax.dot_general(a, b, (((ca,), (cb,)), ((), ())), preferred_element_type=F32)


def coords():
    me = lax.axis_index("band")
    pos = me % SUB
    return me - pos, pos // 8, pos // 4 % 2, pos // 2 % 2, pos % 2


def partners(base, zh, zl, y, c):
    def at(a, b, d, e):
        return {"band": base + a * 8 + b * 4 + d * 2 + e}

    far = at(1 - zh, zl, y, c)
    near = at(zh, 1 - zl, y, c)
    side = at(zh, zl, 1 - y, c)
    core = at(zh, zl, y, 1 - c)
    return far, near, side, core


def greet(devices):
    barrier = pltpu.get_barrier_semaphore()
    for device in devices:
        pl.semaphore_signal(barrier, inc=1, device_id=device, device_id_type=pl.DeviceIdType.MESH)
    pl.semaphore_wait(barrier, len(devices))


def sender(send, recv):
    def copy(src, dst, k, device):
        op = pltpu.make_async_remote_copy(
            src_ref=src,
            dst_ref=dst,
            send_sem=send.at[k],
            recv_sem=recv.at[k],
            device_id=device,
            device_id_type=pl.DeviceIdType.MESH,
        )
        op.start()
        return op

    return copy


def gather_steps(buf, half, copy, first, at, to):
    zh, zl, y, c = at
    far, near, side, core = to
    lo, hi = pl.ds(0, half), pl.ds(half, half)

    def go(ref, k, device):
        return copy(ref, ref, first + k, device)

    ops = [go(buf.at[zh, zl, y, c], 0, far)]
    ops[0].wait_recv()
    ops.append(go(buf.at[:, zl, y, c, lo], 1, side))
    ops.append(go(buf.at[:, zl, y, c, hi], 2, near))
    ops[1].wait_recv()
    ops.append(go(buf.at[:, zl, :, c, lo], 3, near))
    ops[2].wait_recv()
    ops.append(go(buf.at[:, :, y, c, hi], 4, side))
    ops[3].wait_recv()
    ops[4].wait_recv()
    ops.append(go(buf.at[:, :, :, c], 5, core))
    ops[5].wait_recv()
    for op in ops:
        op.wait_send()


def gather_kernel(tok_ref, all_ref, send, recv):
    base, *at = coords()
    to = partners(base, *at)
    zh, zl, y, c = at
    all_ref[zh, zl, y, c] = tok_ref[...]
    greet(to)
    gather_steps(all_ref, tok_ref.shape[0] // 2, sender(send, recv), 0, at, to)


def attend_kernel(
    ids_ref, len_ref, tok_ref, nest_ref, dout_ref, wq_ref, wkv_ref, wo_ref,
    out_ref, dnest_ref, pay_ref,
    pairs, qs, gs, att, dq, dreg, foot, foot_t, qst, gst, pst, dst,
):
    feat = nest_ref.shape[1]
    slots = LIST * GB
    heads = feat // HD
    scale = HD ** (-0.5)
    for i in range(0, SUB * GB, slots):
        pairs[i : i + slots, :] = mm(tok_ref[i : i + slots, :], wkv_ref[...]).astype(BF16)
    dreg[...] = jnp.zeros_like(dreg)
    qs[...] = mm(nest_ref[...], wq_ref[...]).astype(BF16)
    gs[...] = mm(dout_ref[...], wo_ref[...], 1, 1).astype(BF16)
    head_of = lax.broadcasted_iota(jnp.int32, (BT, feat), 1) // HD
    slot_row = lax.broadcasted_iota(jnp.int32, (slots, 2 * BT), 0)

    def block(b, carry):
        rows = pl.ds(pl.multiple_of(b * BT, BT), BT)
        live = len_ref[b] * GB
        for j in range(LIST):
            start = pl.multiple_of(ids_ref[b, j] * GB, GB)
            foot[j * GB : (j + 1) * GB, :] = pairs[pl.ds(start, GB), :]
        foot_t[...] = foot[...].T
        q = qs[rows, :]
        g = gs[rows, :]
        zero = jnp.zeros_like(q)
        for h in range(heads):
            qst[h * BT : (h + 1) * BT, :] = jnp.where(head_of == h, q, zero)
            gst[h * BT : (h + 1) * BT, :] = jnp.where(head_of == h, g, zero)
        att_parts = []
        dq_parts = []
        for hp in range(heads // 2):
            two = slice(hp * 2 * BT, (hp + 1) * 2 * BT)
            s = mm(foot[:, :feat], qst[two, :], 1, 1)
            dp = mm(foot[:, feat:], gst[two, :], 1, 1)
            s = jnp.where(slot_row < live, s, -jnp.inf)
            top = jnp.max(s, axis=0, keepdims=True)
            e = jnp.exp2((s - top) * (scale * math.log2(math.e)))
            p = e * (1.0 / jnp.sum(e, axis=0, keepdims=True))
            p_low = p.astype(BF16)
            pst[:, two] = p_low
            centre = jnp.sum(p * dp, axis=0, keepdims=True)
            d_s = (p * (dp - centre) * scale).astype(BF16)
            dst[:, two] = d_s
            cols = slice(hp * 2 * HD, (hp + 1) * 2 * HD)
            vals = slice(feat + hp * 2 * HD, feat + (hp + 1) * 2 * HD)
            a_t = mm(foot_t[vals, :], p_low)
            q_t = mm(foot_t[cols, :], d_s)
            att_parts += [a_t[:HD, :BT], a_t[HD:, BT:]]
            dq_parts += [q_t[:HD, :BT], q_t[HD:, BT:]]
        att[rows, :] = jnp.concatenate(att_parts, axis=0).T.astype(BF16)
        dq[rows, :] = jnp.concatenate(dq_parts, axis=0).T.astype(BF16)
        d_k = mm(dst[...], qst[...])
        d_v = mm(pst[...], gst[...])
        for j in range(LIST):
            start = pl.multiple_of(ids_ref[b, j] * GB, GB)
            part = slice(j * GB, (j + 1) * GB)
            dreg[pl.ds(start, GB), :feat] += d_k[part, :]
            dreg[pl.ds(start, GB), feat:] += d_v[part, :]
        return carry

    lax.fori_loop(0, nest_ref.shape[0] // BT, block, 0)
    out_ref[...] = mm(att[...], wo_ref[...]).astype(BF16)
    dnest_ref[...] = mm(dq[...], wq_ref[...], 1, 1).astype(BF16)
    w_rows = 2 * feat // SUB
    kv = jnp.zeros((feat, 2 * feat), F32)
    for i in range(0, SUB * GB, slots):
        part = dreg[i : i + slots, :]
        high = part.astype(BF16)
        low = (part - high.astype(F32)).astype(BF16)
        tok = tok_ref[i : i + slots, :]
        kv = kv + mm(tok, high, 0, 0) + mm(tok, low, 0, 0)
        for g in range(LIST):
            pay_ref[i // GB + g, :GB, :] = high[g * GB : (g + 1) * GB, :]
    grad_q = mm(nest_ref[...], dq[...], 0, 0).astype(BF16)
    grad_o = mm(att[...], dout_ref[...], 0, 0).astype(BF16)
    kv = kv.astype(BF16)
    for k in range(SUB // 2):
        part = slice(k * w_rows, (k + 1) * w_rows)
        pay_ref[k, GB:, :] = kv[part, :]
        pay_ref[SUB // 2 + k, GB:, :feat] = grad_q[part, :]
        pay_ref[SUB // 2 + k, GB:, feat:] = grad_o[part, :]


def reduce_kernel(
    norm, pay_ref, wkv_ref, dglob_ref, gq_ref, gkv_ref, go_ref,
    ra, s0, s1, r0, r1, k0, k1, t0, t1, u0, u1, v0, v1, x0, x1, wg, send, recv,
):
    base, *at = coords()
    to = partners(base, *at)
    zh, zl, y, c = at
    far, near, side, core = to
    feat = wkv_ref.shape[0]
    greet(to)
    copy = sender(send, recv)
    left, right = pl.ds(0, feat), pl.ds(feat, feat)
    first = copy(pay_ref.at[:, :, :, 1 - c], ra, 0, core)
    first.wait_recv()
    s0[...] = (
        pay_ref[:, :, 1 - y, c, :, left].astype(F32) + ra[:, :, 1 - y, :, left].astype(F32)
    ).astype(BF16)
    b0 = copy(s0, r0, 1, side)
    s1[...] = (
        pay_ref[:, 1 - zl, :, c, :, right].astype(F32) + ra[:, 1 - zl, :, :, right].astype(F32)
    ).astype(BF16)
    b1 = copy(s1, r1, 2, near)
    k0[...] = pay_ref[:, :, y, c, :, left].astype(F32) + ra[:, :, y, :, left].astype(F32)
    k1[...] = pay_ref[:, zl, :, c, :, right].astype(F32) + ra[:, zl, :, :, right].astype(F32)
    b0.wait_recv()
    t0[...] = (k0[:, 1 - zl] + r0[:, 1 - zl].astype(F32)).astype(BF16)
    c0 = copy(t0, u0, 3, near)
    b1.wait_recv()
    t1[...] = (k1[:, 1 - y] + r1[:, 1 - y].astype(F32)).astype(BF16)
    c1 = copy(t1, u1, 4, side)
    c0.wait_recv()
    v0[...] = (
        k0[1 - zh, zl] + r0[1 - zh, zl].astype(F32) + u0[1 - zh].astype(F32)
    ).astype(BF16)
    d0 = copy(v0, x0, 5, far)
    c1.wait_recv()
    v1[...] = (
        k1[1 - zh, y] + r1[1 - zh, y].astype(F32) + u1[1 - zh].astype(F32)
    ).astype(BF16)
    d1 = copy(v1, x1, 6, far)
    sum0 = k0[zh, zl] + r0[zh, zl].astype(F32) + u0[zh].astype(F32)
    sum1 = k1[zh, y] + r1[zh, y].astype(F32) + u1[zh].astype(F32)
    d0.wait_recv()
    sum0 = sum0 + x0[...].astype(F32)
    wg[zh, zl, y, c, :, left] = sum0[GB:, :].astype(BF16)
    d1.wait_recv()
    sum1 = sum1 + x1[...].astype(F32)
    wg[zh, zl, y, c, :, right] = sum1[GB:, :].astype(BF16)
    total = jnp.zeros((GB, feat), F32)
    for part, cols in ((sum0[:GB, :], left), (sum1[:GB, :], right)):
        high = part.astype(BF16)
        low = (part - high.astype(F32)).astype(BF16)
        w = wkv_ref[:, cols]
        total = total + mm(high, w, 1, 1) + mm(low, w, 1, 1)
    dglob_ref[...] = total.astype(BF16)
    gather_steps(wg, wg.shape[4] // 2, copy, 7, at, to)
    flat = wg[...].astype(F32).reshape(2 * feat, 2 * feat) * norm
    gkv_ref[...] = flat[:feat, :]
    gq_ref[...] = flat[feat:, :feat]
    go_ref[...] = flat[feat:, feat:]
    for op in (first, b0, b1, c0, c1, d0, d1):
        op.wait_send()


def vmem(n):
    return [pl.BlockSpec(memory_space=pltpu.VMEM)] * n


def shards(nest_tokens, global_tokens, block_ids, list_length, w_query, w_keyval, w_out, d_output):
    rows, feat = nest_tokens.shape
    band = lax.axis_size("band")
    device = lax.axis_index("band")
    local_ids = block_ids - (device - device % SUB)
    norm = 1.0 / math.sqrt(rows * band)
    tokens = pl.pallas_call(
        gather_kernel,
        out_shape=jax.ShapeDtypeStruct((2, 2, 2, 2, GB, feat), BF16),
        in_specs=vmem(1),
        out_specs=vmem(1)[0],
        scratch_shapes=[pltpu.SemaphoreType.DMA((6,)), pltpu.SemaphoreType.DMA((6,))],
        compiler_params=pltpu.CompilerParams(
            collective_id=0, has_side_effects=True, vmem_limit_bytes=VMEM_LIMIT
        ),
    )(global_tokens)
    tokens = tokens.reshape(SUB * GB, feat)
    slots = LIST * GB
    wide = feat // HD * BT
    depth = GB + 2 * feat // SUB
    smem = [pl.BlockSpec(memory_space=pltpu.SMEM)] * 2
    output, d_nest, payload = pl.pallas_call(
        attend_kernel,
        out_shape=(
            jax.ShapeDtypeStruct((rows, feat), BF16),
            jax.ShapeDtypeStruct((rows, feat), BF16),
            jax.ShapeDtypeStruct((SUB, depth, 2 * feat), BF16),
        ),
        in_specs=smem + vmem(6),
        out_specs=tuple(vmem(3)),
        scratch_shapes=[
            pltpu.VMEM((SUB * GB, 2 * feat), BF16),
            pltpu.VMEM((rows, feat), BF16),
            pltpu.VMEM((rows, feat), BF16),
            pltpu.VMEM((rows, feat), BF16),
            pltpu.VMEM((rows, feat), BF16),
            pltpu.VMEM((SUB * GB, 2 * feat), F32),
            pltpu.VMEM((slots, 2 * feat), BF16),
            pltpu.VMEM((2 * feat, slots), BF16),
            pltpu.VMEM((wide, feat), BF16),
            pltpu.VMEM((wide, feat), BF16),
            pltpu.VMEM((slots, wide), BF16),
            pltpu.VMEM((slots, wide), BF16),
        ],
        compiler_params=pltpu.CompilerParams(vmem_limit_bytes=VMEM_LIMIT),
    )(local_ids, list_length, tokens, nest_tokens, d_output, w_query, w_keyval, w_out)
    payload = payload.reshape(2, 2, 2, 2, depth, 2 * feat)
    d_global, grad_q, grad_kv, grad_o = pl.pallas_call(
        functools.partial(reduce_kernel, norm),
        out_shape=(
            jax.ShapeDtypeStruct((GB, feat), BF16),
            jax.ShapeDtypeStruct((feat, feat), F32),
            jax.ShapeDtypeStruct((feat, 2 * feat), F32),
            jax.ShapeDtypeStruct((feat, feat), F32),
        ),
        in_specs=vmem(2),
        out_specs=tuple(vmem(4)),
        scratch_shapes=[
            pltpu.VMEM((2, 2, 2, depth, 2 * feat), BF16),
            pltpu.VMEM((2, 2, depth, feat), BF16),
            pltpu.VMEM((2, 2, depth, feat), BF16),
            pltpu.VMEM((2, 2, depth, feat), BF16),
            pltpu.VMEM((2, 2, depth, feat), BF16),
            pltpu.VMEM((2, 2, depth, feat), F32),
            pltpu.VMEM((2, 2, depth, feat), F32),
            pltpu.VMEM((2, depth, feat), BF16),
            pltpu.VMEM((2, depth, feat), BF16),
            pltpu.VMEM((2, depth, feat), BF16),
            pltpu.VMEM((2, depth, feat), BF16),
            pltpu.VMEM((depth, feat), BF16),
            pltpu.VMEM((depth, feat), BF16),
            pltpu.VMEM((depth, feat), BF16),
            pltpu.VMEM((depth, feat), BF16),
            pltpu.VMEM((2, 2, 2, 2, depth - GB, 2 * feat), BF16),
            pltpu.SemaphoreType.DMA((13,)),
            pltpu.SemaphoreType.DMA((13,)),
        ],
        compiler_params=pltpu.CompilerParams(
            collective_id=1, has_side_effects=True, vmem_limit_bytes=VMEM_LIMIT
        ),
    )(payload, w_keyval)
    if band > SUB:
        groups = [[s + SUB * k for k in range(band // SUB)] for s in range(SUB)]
        grad_q, grad_kv, grad_o = lax.psum(
            (grad_q, grad_kv, grad_o), "band", axis_index_groups=groups
        )
    return output, d_nest, d_global, grad_q, grad_kv, grad_o


def solution(mesh):
    both = ("groups", "band")
    in_specs = (
        P(both, None), P(both, None), P(both, None), P(both), P(), P(), P(), P(both, None),
    )
    out_specs = (
        P(both, None), P(both, None), P(both, None),
        P("groups", None), P("groups", None), P("groups", None),
    )
    return jax.shard_map(shards, mesh=mesh, in_specs=in_specs, out_specs=out_specs, check_vma=False)
```

time: 376 us -> 89.2 us (0.24)
  waiting for transfers between devices: 207 us -> 0 us
  matrix products: 88.4 us -> 0 us
  Pallas kernels: 0 us -> 80.2 us
  other arithmetic: 29.7 us -> 1.26 us
  local copies, waits for them, and re-layouts: 27.7 us -> 6.68 us
  between operations: 14.4 us -> 0.66 us
  starting transfers between devices: 8.2 us -> 0 us
    ppermute x8 -> x0, waiting for transfers between devices: 116 us -> none  [from_partner(): return lax.ppermute(block, axis, route)]
    psum x1 -> x0, waiting for transfers between devices: 90.5 us -> none  [shards(): lax.psum((query_term, keyval_term, out_term), 'band')]
    dot_general x15 -> x0, matrix products: 88.4 us -> none  [the longest x1 34.5 us: attend_block(): jnp.einsum('hqk,qhd->khd', d_scores, queries, preferred_element_type=jnp....]
    pallas_call x0 -> x3, Pallas kernels: none -> 80.2 us  [the longest x1 42.3 us: shards(): pl.pallas_call(functools.partial(reduce_kernel, norm), out_shape=(jax.Sha...]
    scatter-add x1 -> x0, other arithmetic: 9.93 us -> none  [visit(): carry.at[id_group.reshape(-1)].add(d_foot.reshape(-1, GB, 2 * features))]
    concatenate x3 -> x0, local copies, waits for them, and re-layouts: 9.07 us -> none  [attend_block(): jnp.concatenate([d_keys, d_values], axis=-1)]
    ppermute x8 -> x0, starting transfers between devices: 8.16 us -> none  [from_partner(): return lax.ppermute(block, axis, route)]
    concatenate x1 -> x0, other arithmetic: 4.44 us -> none  [attend_block(): jnp.concatenate([d_keys, d_values], axis=-1)]
  transfers between devices with their start and end apart: 9 -> 0, of which waited for: 8 -> 0; matrix products, arithmetic and copies ran while one was open for 12% -> 0% of each run, Pallas kernels for 0% -> 0%
where the time goes in v1:
time: 89.2 us; the launch traced here: 88.8 us
  Pallas kernels  80.2 us (90%)
  local copies, waits for them, and re-layouts  6.68 us (7%)
  other arithmetic  1.26 us (1%)
    pallas_call x1, Pallas kernels, shards(): pl.pallas_call(functools.partial(reduce_kernel, norm), out_shape=(jax.Sha...  42.3 us
    pallas_call x1, Pallas kernels, shards(): pl.pallas_call(gather_kernel, out_shape=jax.ShapeDtypeStruct((2, 2, 2, 2,...  19.8 us
    pallas_call x1, Pallas kernels, shards(): pl.pallas_call(attend_kernel, out_shape=(jax.ShapeDtypeStruct((rows, feat...  18.1 us
    unnamed x4, local copies, waits for them, and re-layouts  6.68 us

profile of v1, /device:TPU:0, one launch (start us, length us, event | category | flops | bytes accessed | tf_op | source)
XLA Modules:
  0.0 88.8 jit_solution(13014213485351611391)
XLA Ops:
  0.6 1.3 %broadcast_subtract_fusion.ids_ref = s32[4,4]{1,0:T(4,128)} fusion(s32[4,4]{1,0:T(4,128)} %param.10, s32[]{:T(128)S(6)} %sub.9), kind=kLoop, calls=%fused_computation | loop fusion | flops 16 | bytes 132 | tf_op jit(solution)/shard_map/sub | solution.py:255
  1.9 19.8 %shard_map.127 = bf16[2,2,2,2,128,256]{5,4,3,2,1,0:T(8,128)(2,1)} custom-call(bf16[128,256]{1,0:T(8,128)(2,1)} %tok_ref.1), custom_call_target="tpu_custom_call" | custom-call | tf_op jit(solution)/shard_map/pallas_call | solution.py:257
  21.7 18.1 %shard_map.128 = (bf16[512,256]{1,0:T(8,128)(2,1)}, bf16[512,256]{1,0:T(8,128)(2,1)}, bf16[16,160,512]{2,1,0:T(8,128)(2,1)}) custom-call(s32[4,4]{1,0:T(4,128)} %broadcast_subtract_fusion.ids_ref, s32[4]{0:T(128)} %len_ref.1, bf16[2048,256]{1,0:T(8,128)(2,1)} %bitcast.2, bf16[512,256]{1,0:T(8,128)(2,1)} %nest_ref.1, bf16[512,256]{1,0:T(8,128)(2,1)} %dout_ref.1, ...), custom_call_target="tpu_custom_call" | custom-call | tf_op jit(solution)/shard_map/pallas_call | solution.py:272
  39.8 42.3 %shard_map.129 = (bf16[128,256]{1,0:T(8,128)(2,1)}, f32[256,256]{1,0:T(8,128)}, f32[256,512]{1,0:T(8,128)}, f32[256,256]{1,0:T(8,128)}) custom-call(bf16[2,2,2,2,160,512]{5,4,3,2,1,0:T(8,128)(2,1)} %bitcast.3, bf16[256,512]{1,0:T(8,128)(2,1)} %wkv_ref.3), custom_call_target="tpu_custom_call" | custom-call | tf_op jit(solution)/shard_map/pallas_call | solution.py:298
  82.2 1.5 %copy.18 = bf16[128,256]{1,0:T(8,128)(2,1)} copy(bf16[128,256]{1,0:T(8,128)(2,1)} %get-tuple-element.28) | data formatting | bytes 131072
  83.6 1.7 %copy.19 = f32[256,256]{1,0:T(8,128)} copy(f32[256,256]{1,0:T(8,128)} %get-tuple-element.29) | data formatting | bytes 524288
  85.3 1.9 %copy.20 = f32[256,512]{1,0:T(8,128)} copy(f32[256,512]{1,0:T(8,128)} %get-tuple-element.30) | data formatting | bytes 1048576
  87.2 1.7 %copy.21 = f32[256,256]{1,0:T(8,128)} copy(f32[256,256]{1,0:T(8,128)} %get-tuple-element.31) | data formatting | bytes 524288

commit v2 on v1

--- a/solution.py
+++ b/solution.py
@@ -62,7 +62,7 @@
     return copy
 
 
-def gather_steps(buf, half, copy, first, at, to):
+def gather_steps(buf, half, copy, first, at, to, beside=None):
     zh, zl, y, c = at
     far, near, side, core = to
     lo, hi = pl.ds(0, half), pl.ds(half, half)
@@ -71,6 +71,8 @@
         return copy(ref, ref, first + k, device)
 
     ops = [go(buf.at[zh, zl, y, c], 0, far)]
+    if beside is not None:
+        beside()
     ops[0].wait_recv()
     ops.append(go(buf.at[:, zl, y, c, lo], 1, side))
     ops.append(go(buf.at[:, zl, y, c, hi], 2, near))
@@ -116,7 +118,7 @@
         rows = pl.ds(pl.multiple_of(b * BT, BT), BT)
         live = len_ref[b] * GB
         for j in range(LIST):
-            start = pl.multiple_of(ids_ref[b, j] * GB, GB)
+            start = pl.multiple_of(lax.rem(ids_ref[b, j], SUB) * GB, GB)
             foot[j * GB : (j + 1) * GB, :] = pairs[pl.ds(start, GB), :]
         foot_t[...] = foot[...].T
         q = qs[rows, :]
@@ -151,7 +153,7 @@
         d_k = mm(dst[...], qst[...])
         d_v = mm(pst[...], gst[...])
         for j in range(LIST):
-            start = pl.multiple_of(ids_ref[b, j] * GB, GB)
+            start = pl.multiple_of(lax.rem(ids_ref[b, j], SUB) * GB, GB)
             part = slice(j * GB, (j + 1) * GB)
             dreg[pl.ds(start, GB), :feat] += d_k[part, :]
             dreg[pl.ds(start, GB), feat:] += d_v[part, :]
@@ -169,79 +171,92 @@
         tok = tok_ref[i : i + slots, :]
         kv = kv + mm(tok, high, 0, 0) + mm(tok, low, 0, 0)
         for g in range(LIST):
-            pay_ref[i // GB + g, :GB, :] = high[g * GB : (g + 1) * GB, :]
+            for n in range(2 * feat // CH):
+                pay_ref[n, i // GB + g, :GB, :] = high[
+                    g * GB : (g + 1) * GB, n * CH : (n + 1) * CH
+                ]
     grad_q = mm(nest_ref[...], dq[...], 0, 0).astype(BF16)
     grad_o = mm(att[...], dout_ref[...], 0, 0).astype(BF16)
     kv = kv.astype(BF16)
+    per = feat // CH
     for k in range(SUB // 2):
         part = slice(k * w_rows, (k + 1) * w_rows)
-        pay_ref[k, GB:, :] = kv[part, :]
-        pay_ref[SUB // 2 + k, GB:, :feat] = grad_q[part, :]
-        pay_ref[SUB // 2 + k, GB:, feat:] = grad_o[part, :]
+        for n in range(2 * per):
+            cols = slice(n % per * CH, (n % per + 1) * CH)
+            pay_ref[n, k, GB:, :] = kv[part, n * CH : (n + 1) * CH]
+            pay_ref[n, SUB // 2 + k, GB:, :] = (grad_q if n < per else grad_o)[part, cols]
+
+
+CH = 128
 
 
 def reduce_kernel(
-    norm, pay_ref, wkv_ref, dglob_ref, gq_ref, gkv_ref, go_ref,
-    ra, s0, s1, r0, r1, k0, k1, t0, t1, u0, u1, v0, v1, x0, x1, wg, send, recv,
+    pay_ref, wkv_ref, dglob_ref, wg,
+    ra, s_buf, r_buf, kept, t_buf, u_buf, v_buf, x_buf, own, send, recv,
 ):
     base, *at = coords()
     to = partners(base, *at)
     zh, zl, y, c = at
     far, near, side, core = to
     feat = wkv_ref.shape[0]
+    chunks = pay_ref.shape[0]
+    order = [k // 2 + k % 2 * (chunks // 2) for k in range(chunks)]
     greet(to)
     copy = sender(send, recv)
-    left, right = pl.ds(0, feat), pl.ds(feat, feat)
-    first = copy(pay_ref.at[:, :, :, 1 - c], ra, 0, core)
-    first.wait_recv()
-    s0[...] = (
-        pay_ref[:, :, 1 - y, c, :, left].astype(F32) + ra[:, :, 1 - y, :, left].astype(F32)
-    ).astype(BF16)
-    b0 = copy(s0, r0, 1, side)
-    s1[...] = (
-        pay_ref[:, 1 - zl, :, c, :, right].astype(F32) + ra[:, 1 - zl, :, :, right].astype(F32)
-    ).astype(BF16)
-    b1 = copy(s1, r1, 2, near)
-    k0[...] = pay_ref[:, :, y, c, :, left].astype(F32) + ra[:, :, y, :, left].astype(F32)
-    k1[...] = pay_ref[:, zl, :, c, :, right].astype(F32) + ra[:, zl, :, :, right].astype(F32)
-    b0.wait_recv()
-    t0[...] = (k0[:, 1 - zl] + r0[:, 1 - zl].astype(F32)).astype(BF16)
-    c0 = copy(t0, u0, 3, near)
-    b1.wait_recv()
-    t1[...] = (k1[:, 1 - y] + r1[:, 1 - y].astype(F32)).astype(BF16)
-    c1 = copy(t1, u1, 4, side)
-    c0.wait_recv()
-    v0[...] = (
-        k0[1 - zh, zl] + r0[1 - zh, zl].astype(F32) + u0[1 - zh].astype(F32)
-    ).astype(BF16)
-    d0 = copy(v0, x0, 5, far)
-    c1.wait_recv()
-    v1[...] = (
-        k1[1 - zh, y] + r1[1 - zh, y].astype(F32) + u1[1 - zh].astype(F32)
-    ).astype(BF16)
-    d1 = copy(v1, x1, 6, far)
-    sum0 = k0[zh, zl] + r0[zh, zl].astype(F32) + u0[zh].astype(F32)
-    sum1 = k1[zh, y] + r1[zh, y].astype(F32) + u1[zh].astype(F32)
-    d0.wait_recv()
-    sum0 = sum0 + x0[...].astype(F32)
-    wg[zh, zl, y, c, :, left] = sum0[GB:, :].astype(BF16)
-    d1.wait_recv()
-    sum1 = sum1 + x1[...].astype(F32)
-    wg[zh, zl, y, c, :, right] = sum1[GB:, :].astype(BF16)
-    total = jnp.zeros((GB, feat), F32)
-    for part, cols in ((sum0[:GB, :], left), (sum1[:GB, :], right)):
+    ops = [copy(pay_ref.at[k, :, :, :, 1 - c], ra.at[k], k, core) for k in order]
+    ops_a = dict(zip(order, ops))
+    ops_b, ops_c, ops_d = {}, {}, {}
+    for k in order:
+        ops_a[k].wait_recv()
+        if k < chunks // 2:
+            sent = pay_ref[k, :, :, 1 - y, c].astype(F32) + ra[k, :, :, 1 - y].astype(F32)
+            s_buf[k] = sent.astype(BF16)
+            ops_b[k] = copy(s_buf.at[k], r_buf.at[k], chunks + k, side)
+            kept[k] = pay_ref[k, :, :, y, c].astype(F32) + ra[k, :, :, y].astype(F32)
+        else:
+            sent = pay_ref[k, :, 1 - zl, :, c].astype(F32) + ra[k, :, 1 - zl].astype(F32)
+            s_buf[k] = sent.astype(BF16)
+            ops_b[k] = copy(s_buf.at[k], r_buf.at[k], chunks + k, near)
+            kept[k] = pay_ref[k, :, zl, :, c].astype(F32) + ra[k, :, zl].astype(F32)
+    for k in order:
+        mine, there = (zl, near) if k < chunks // 2 else (y, side)
+        ops_b[k].wait_recv()
+        t_buf[k] = (kept[k, :, 1 - mine] + r_buf[k, :, 1 - mine].astype(F32)).astype(BF16)
+        ops_c[k] = copy(t_buf.at[k], u_buf.at[k], 2 * chunks + k, there)
+    for k in order:
+        mine = zl if k < chunks // 2 else y
+        ops_c[k].wait_recv()
+        v_buf[k] = (
+            kept[k, 1 - zh, mine] + r_buf[k, 1 - zh, mine].astype(F32) + u_buf[k, 1 - zh].astype(F32)
+        ).astype(BF16)
+        ops_d[k] = copy(v_buf.at[k], x_buf.at[k], 3 * chunks + k, far)
+    for k in order:
+        mine = zl if k < chunks // 2 else y
+        part = kept[k, zh, mine] + r_buf[k, zh, mine].astype(F32) + u_buf[k, zh].astype(F32)
+        ops_d[k].wait_recv()
+        part = part + x_buf[k].astype(F32)
+        wg[zh, zl, y, c, :, k * CH : (k + 1) * CH] = part[GB:, :].astype(BF16)
+        own[:, k * CH : (k + 1) * CH] = part[:GB, :]
+
+    def finish():
+        part = own[...]
         high = part.astype(BF16)
         low = (part - high.astype(F32)).astype(BF16)
-        w = wkv_ref[:, cols]
-        total = total + mm(high, w, 1, 1) + mm(low, w, 1, 1)
-    dglob_ref[...] = total.astype(BF16)
-    gather_steps(wg, wg.shape[4] // 2, copy, 7, at, to)
-    flat = wg[...].astype(F32).reshape(2 * feat, 2 * feat) * norm
-    gkv_ref[...] = flat[:feat, :]
-    gq_ref[...] = flat[feat:, :feat]
-    go_ref[...] = flat[feat:, feat:]
-    for op in (first, b0, b1, c0, c1, d0, d1):
-        op.wait_send()
+        total = mm(high, wkv_ref[...], 1, 1) + mm(low, wkv_ref[...], 1, 1)
+        dglob_ref[...] = total.astype(BF16)
+
+    gather_steps(wg, wg.shape[4] // 2, copy, 4 * chunks, at, to, finish)
+    for group in (ops_a, ops_b, ops_c, ops_d):
+        for k in order:
+            group[k].wait_send()
+
+
+def finish_kernel(norm, dglob_in, wg_ref, dglob_ref, gq_ref, gkv_ref, go_ref):
+    feat = gq_ref.shape[0]
+    dglob_ref[...] = dglob_in[...]
+    gkv_ref[...] = wg_ref[:feat, :].astype(F32) * norm
+    gq_ref[...] = wg_ref[feat:, :feat].astype(F32) * norm
+    go_ref[...] = wg_ref[feat:, feat:].astype(F32) * norm
 
 
 def vmem(n):
@@ -251,8 +266,6 @@
 def shards(nest_tokens, global_tokens, block_ids, list_length, w_query, w_keyval, w_out, d_output):
     rows, feat = nest_tokens.shape
     band = lax.axis_size("band")
-    device = lax.axis_index("band")
-    local_ids = block_ids - (device - device % SUB)
     norm = 1.0 / math.sqrt(rows * band)
     tokens = pl.pallas_call(
         gather_kernel,
@@ -274,7 +287,7 @@
         out_shape=(
             jax.ShapeDtypeStruct((rows, feat), BF16),
             jax.ShapeDtypeStruct((rows, feat), BF16),
-            jax.ShapeDtypeStruct((SUB, depth, 2 * feat), BF16),
+            jax.ShapeDtypeStruct((2 * feat // CH, SUB, depth, CH), BF16),
         ),
         in_specs=smem + vmem(6),
         out_specs=tuple(vmem(3)),
@@ -293,10 +306,36 @@
             pltpu.VMEM((slots, wide), BF16),
         ],
         compiler_params=pltpu.CompilerParams(vmem_limit_bytes=VMEM_LIMIT),
-    )(local_ids, list_length, tokens, nest_tokens, d_output, w_query, w_keyval, w_out)
-    payload = payload.reshape(2, 2, 2, 2, depth, 2 * feat)
+    )(block_ids, list_length, tokens, nest_tokens, d_output, w_query, w_keyval, w_out)
+    n = 2 * feat // CH
+    payload = payload.reshape(n, 2, 2, 2, 2, depth, CH)
+    d_global, sums = pl.pallas_call(
+        reduce_kernel,
+        out_shape=(
+            jax.ShapeDtypeStruct((GB, feat), BF16),
+            jax.ShapeDtypeStruct((2, 2, 2, 2, depth - GB, 2 * feat), BF16),
+        ),
+        in_specs=vmem(2),
+        out_specs=tuple(vmem(2)),
+        scratch_shapes=[
+            pltpu.VMEM((n, 2, 2, 2, depth, CH), BF16),
+            pltpu.VMEM((n, 2, 2, depth, CH), BF16),
+            pltpu.VMEM((n, 2, 2, depth, CH), BF16),
+            pltpu.VMEM((n, 2, 2, depth, CH), F32),
+            pltpu.VMEM((n, 2, depth, CH), BF16),
+            pltpu.VMEM((n, 2, depth, CH), BF16),
+            pltpu.VMEM((n, depth, CH), BF16),
+            pltpu.VMEM((n, depth, CH), BF16),
+            pltpu.VMEM((GB, 2 * feat), F32),
+            pltpu.SemaphoreType.DMA((4 * n + 6,)),
+            pltpu.SemaphoreType.DMA((4 * n + 6,)),
+        ],
+        compiler_params=pltpu.CompilerParams(
+            collective_id=1, has_side_effects=True, vmem_limit_bytes=VMEM_LIMIT
+        ),
+    )(payload, w_keyval)
     d_global, grad_q, grad_kv, grad_o = pl.pallas_call(
-        functools.partial(reduce_kernel, norm),
+        functools.partial(finish_kernel, norm),
         out_shape=(
             jax.ShapeDtypeStruct((GB, feat), BF16),
             jax.ShapeDtypeStruct((feat, feat), F32),
@@ -305,30 +344,8 @@
         ),
         in_specs=vmem(2),
         out_specs=tuple(vmem(4)),
-        scratch_shapes=[
-            pltpu.VMEM((2, 2, 2, depth, 2 * feat), BF16),
-            pltpu.VMEM((2, 2, depth, feat), BF16),
-            pltpu.VMEM((2, 2, depth, feat), BF16),
-            pltpu.VMEM((2, 2, depth, feat), BF16),
-            pltpu.VMEM((2, 2, depth, feat), BF16),
-            pltpu.VMEM((2, 2, depth, feat), F32),
-            pltpu.VMEM((2, 2, depth, feat), F32),
-            pltpu.VMEM((2, depth, feat), BF16),
-            pltpu.VMEM((2, depth, feat), BF16),
-            pltpu.VMEM((2, depth, feat), BF16),
-            pltpu.VMEM((2, depth, feat), BF16),
-            pltpu.VMEM((depth, feat), BF16),
-            pltpu.VMEM((depth, feat), BF16),
-            pltpu.VMEM((depth, feat), BF16),
-            pltpu.VMEM((depth, feat), BF16),
-            pltpu.VMEM((2, 2, 2, 2, depth - GB, 2 * feat), BF16),
-            pltpu.SemaphoreType.DMA((13,)),
-            pltpu.SemaphoreType.DMA((13,)),
-        ],
-        compiler_params=pltpu.CompilerParams(
-            collective_id=1, has_side_effects=True, vmem_limit_bytes=VMEM_LIMIT
-        ),
-    )(payload, w_keyval)
+        compiler_params=pltpu.CompilerParams(vmem_limit_bytes=VMEM_LIMIT),
+    )(d_global, sums.reshape(2 * feat, 2 * feat))
     if band > SUB:
         groups = [[s + SUB * k for k in range(band // SUB)] for s in range(SUB)]
         grad_q, grad_kv, grad_o = lax.psum(

time: 89.2 us -> 78.7 us (0.88)
  local copies, waits for them, and re-layouts: 6.68 us -> 0 us
  Pallas kernels: 80.2 us -> 77.8 us
  other arithmetic: 1.26 us -> 0 us
    unnamed x4 -> x0, local copies, waits for them, and re-layouts: 6.68 us -> none
    pallas_call x1 -> x2, Pallas kernels: 42.3 us -> 39.8 us  [the longest x1 37.7 us: shards(): pl.pallas_call(reduce_kernel, out_shape=(jax.ShapeDtypeStruct((GB, feat),...]
    sub x1 -> x0, other arithmetic: 1.26 us -> none  [shards(): local_ids = block_ids - (device - device % SUB)]
where the time goes in v2:
time: 78.7 us; the launch traced here: 78.4 us
  Pallas kernels  77.8 us (99%)
    pallas_call x1, Pallas kernels, shards(): pl.pallas_call(reduce_kernel, out_shape=(jax.ShapeDtypeStruct((GB, feat),...  37.7 us
    pallas_call x1, Pallas kernels, shards(): pl.pallas_call(gather_kernel, out_shape=jax.ShapeDtypeStruct((2, 2, 2, 2,...  19.8 us
    pallas_call x1, Pallas kernels, shards(): pl.pallas_call(attend_kernel, out_shape=(jax.ShapeDtypeStruct((rows, feat...  18.2 us
    pallas_call x1, Pallas kernels, shards(): pl.pallas_call(functools.partial(finish_kernel, norm), out_shape=(jax.Sha...  2.12 us

profile of v2, /device:TPU:0, one launch (start us, length us, event | category | flops | bytes accessed | tf_op | source)
XLA Modules:
  0.0 78.4 jit_solution(17502344306212787033)
XLA Ops:
  0.6 19.8 %shard_map.127 = bf16[2,2,2,2,128,256]{5,4,3,2,1,0:T(8,128)(2,1)} custom-call(bf16[128,256]{1,0:T(8,128)(2,1)} %tok_ref.1), custom_call_target="tpu_custom_call" | custom-call | tf_op jit(solution)/shard_map/pallas_call | solution.py:270
  20.4 18.2 %shard_map.128 = (bf16[512,256]{1,0:T(8,128)(2,1)}, bf16[512,256]{1,0:T(8,128)(2,1)}, bf16[4,16,160,128]{3,2,1,0:T(8,128)(2,1)}) custom-call(s32[4,4]{1,0:T(4,128)} %ids_ref.1, s32[4]{0:T(128)} %len_ref.1, bf16[2048,256]{1,0:T(8,128)(2,1)} %bitcast.3, bf16[512,256]{1,0:T(8,128)(2,1)} %nest_ref.1, bf16[512,256]{1,0:T(8,128)(2,1)} %dout_ref.1, ...), custom_call_target="tpu_custom_call" | custom-call | tf_op jit(solution)/shard_map/pallas_call | solution.py:285
  38.6 37.7 %shard_map.129 = (bf16[128,256]{1,0:T(8,128)(2,1)}, bf16[2,2,2,2,32,512]{5,4,3,2,1,0:T(8,128)(2,1)}) custom-call(bf16[4,2,2,2,2,160,128]{6,5,4,3,2,1,0:T(8,128)(2,1)} %bitcast.4, bf16[256,512]{1,0:T(8,128)(2,1)} %wkv_ref.3), custom_call_target="tpu_custom_call" | custom-call | tf_op jit(solution)/shard_map/pallas_call | solution.py:312
  76.3 2.1 %shard_map.130 = (bf16[128,256]{1,0:T(8,128)(2,1)}, f32[256,256]{1,0:T(8,128)}, f32[256,512]{1,0:T(8,128)}, f32[256,256]{1,0:T(8,128)}) custom-call(bf16[128,256]{1,0:T(8,128)(2,1)} %get-tuple-element.18.dglob_in, bf16[512,512]{1,0:T(8,128)(2,1)} %bitcast.5), custom_call_target="tpu_custom_call" | custom-call | tf_op jit(solution)/shard_map/pallas_call | solution.py:337

commit v3 on v2

--- a/solution.py
+++ b/solution.py
@@ -62,7 +62,7 @@
     return copy
 
 
-def gather_steps(buf, half, copy, first, at, to, beside=None):
+def gather_steps(buf, half, copy, first, at, to):
     zh, zl, y, c = at
     far, near, side, core = to
     lo, hi = pl.ds(0, half), pl.ds(half, half)
@@ -71,21 +71,62 @@
         return copy(ref, ref, first + k, device)
 
     ops = [go(buf.at[zh, zl, y, c], 0, far)]
-    if beside is not None:
-        beside()
+    yield
     ops[0].wait_recv()
     ops.append(go(buf.at[:, zl, y, c, lo], 1, side))
     ops.append(go(buf.at[:, zl, y, c, hi], 2, near))
+    yield
     ops[1].wait_recv()
     ops.append(go(buf.at[:, zl, :, c, lo], 3, near))
     ops[2].wait_recv()
     ops.append(go(buf.at[:, :, y, c, hi], 4, side))
+    yield
     ops[3].wait_recv()
     ops[4].wait_recv()
     ops.append(go(buf.at[:, :, :, c], 5, core))
+    yield
     ops[5].wait_recv()
     for op in ops:
         op.wait_send()
+    yield
+
+
+def halve_steps(side_first, pay, bufs, copy, k, at, to, done):
+    ra, s_buf, r_buf, kept, t_buf, u_buf, v_buf, x_buf = bufs
+    zh, zl, y, c = at
+    far, near, side, core = to
+    ops = [copy(pay.at[:, :, :, 1 - c], ra, k, core)]
+    yield
+    ops[0].wait_recv()
+    if side_first:
+        sent = pay[:, :, 1 - y, c].astype(F32) + ra[:, :, 1 - y].astype(F32)
+    else:
+        sent = pay[:, 1 - zl, :, c].astype(F32) + ra[:, 1 - zl].astype(F32)
+    s_buf[...] = sent.astype(BF16)
+    ops.append(copy(s_buf, r_buf, k + 1, side if side_first else near))
+    if side_first:
+        kept[...] = pay[:, :, y, c].astype(F32) + ra[:, :, y].astype(F32)
+    else:
+        kept[...] = pay[:, zl, :, c].astype(F32) + ra[:, zl].astype(F32)
+    mine = zl if side_first else y
+    yield
+    ops[1].wait_recv()
+    t_buf[...] = (kept[:, 1 - mine] + r_buf[:, 1 - mine].astype(F32)).astype(BF16)
+    ops.append(copy(t_buf, u_buf, k + 2, near if side_first else side))
+    yield
+    ops[2].wait_recv()
+    v_buf[...] = (
+        kept[1 - zh, mine] + r_buf[1 - zh, mine].astype(F32) + u_buf[1 - zh].astype(F32)
+    ).astype(BF16)
+    ops.append(copy(v_buf, x_buf, k + 3, far))
+    yield
+    ops[3].wait_recv()
+    part = kept[zh, mine] + r_buf[zh, mine].astype(F32) + u_buf[zh].astype(F32)
+    done(part + x_buf[...].astype(F32))
+    yield
+    for op in ops:
+        op.wait_send()
+    yield
 
 
 def gather_kernel(tok_ref, all_ref, send, recv):
@@ -94,12 +135,13 @@
     zh, zl, y, c = at
     all_ref[zh, zl, y, c] = tok_ref[...]
     greet(to)
-    gather_steps(all_ref, tok_ref.shape[0] // 2, sender(send, recv), 0, at, to)
+    for _ in gather_steps(all_ref, tok_ref.shape[0] // 2, sender(send, recv), 0, at, to):
+        pass
 
 
 def attend_kernel(
     ids_ref, len_ref, tok_ref, nest_ref, dout_ref, wq_ref, wkv_ref, wo_ref,
-    out_ref, dnest_ref, pay_ref,
+    out_ref, dnest_ref, pay_ref, wpay_ref,
     pairs, qs, gs, att, dq, dreg, foot, foot_t, qst, gst, pst, dst,
 ):
     feat = nest_ref.shape[1]
@@ -172,83 +214,95 @@
         kv = kv + mm(tok, high, 0, 0) + mm(tok, low, 0, 0)
         for g in range(LIST):
             for n in range(2 * feat // CH):
-                pay_ref[n, i // GB + g, :GB, :] = high[
+                pay_ref[n, i // GB + g] = high[
                     g * GB : (g + 1) * GB, n * CH : (n + 1) * CH
                 ]
     grad_q = mm(nest_ref[...], dq[...], 0, 0).astype(BF16)
     grad_o = mm(att[...], dout_ref[...], 0, 0).astype(BF16)
     kv = kv.astype(BF16)
-    per = feat // CH
     for k in range(SUB // 2):
         part = slice(k * w_rows, (k + 1) * w_rows)
-        for n in range(2 * per):
-            cols = slice(n % per * CH, (n % per + 1) * CH)
-            pay_ref[n, k, GB:, :] = kv[part, n * CH : (n + 1) * CH]
-            pay_ref[n, SUB // 2 + k, GB:, :] = (grad_q if n < per else grad_o)[part, cols]
+        wpay_ref[0, k] = kv[part, :feat]
+        wpay_ref[1, k] = kv[part, feat:]
+        wpay_ref[0, SUB // 2 + k] = grad_q[part, :]
+        wpay_ref[1, SUB // 2 + k] = grad_o[part, :]
 
 
 CH = 128
 
 
-def reduce_kernel(
-    pay_ref, wkv_ref, dglob_ref, wg,
-    ra, s_buf, r_buf, kept, t_buf, u_buf, v_buf, x_buf, own, send, recv,
-):
+def reduce_kernel(pay_ref, wpay_ref, wkv_ref, dglob_ref, wg, *rest):
+    pair_bufs, weight_bufs, (own, send, recv) = rest[:8], rest[8:16], rest[16:]
     base, *at = coords()
     to = partners(base, *at)
     zh, zl, y, c = at
-    far, near, side, core = to
     feat = wkv_ref.shape[0]
     chunks = pay_ref.shape[0]
-    order = [k // 2 + k % 2 * (chunks // 2) for k in range(chunks)]
     greet(to)
     copy = sender(send, recv)
-    ops = [copy(pay_ref.at[k, :, :, :, 1 - c], ra.at[k], k, core) for k in order]
-    ops_a = dict(zip(order, ops))
-    ops_b, ops_c, ops_d = {}, {}, {}
-    for k in order:
-        ops_a[k].wait_recv()
-        if k < chunks // 2:
-            sent = pay_ref[k, :, :, 1 - y, c].astype(F32) + ra[k, :, :, 1 - y].astype(F32)
-            s_buf[k] = sent.astype(BF16)
-            ops_b[k] = copy(s_buf.at[k], r_buf.at[k], chunks + k, side)
-            kept[k] = pay_ref[k, :, :, y, c].astype(F32) + ra[k, :, :, y].astype(F32)
-        else:
-            sent = pay_ref[k, :, 1 - zl, :, c].astype(F32) + ra[k, :, 1 - zl].astype(F32)
-            s_buf[k] = sent.astype(BF16)
-            ops_b[k] = copy(s_buf.at[k], r_buf.at[k], chunks + k, near)
-            kept[k] = pay_ref[k, :, zl, :, c].astype(F32) + ra[k, :, zl].astype(F32)
-    for k in order:
-        mine, there = (zl, near) if k < chunks // 2 else (y, side)
-        ops_b[k].wait_recv()
-        t_buf[k] = (kept[k, :, 1 - mine] + r_buf[k, :, 1 - mine].astype(F32)).astype(BF16)
-        ops_c[k] = copy(t_buf.at[k], u_buf.at[k], 2 * chunks + k, there)
-    for k in order:
-        mine = zl if k < chunks // 2 else y
-        ops_c[k].wait_recv()
-        v_buf[k] = (
-            kept[k, 1 - zh, mine] + r_buf[k, 1 - zh, mine].astype(F32) + u_buf[k, 1 - zh].astype(F32)
-        ).astype(BF16)
-        ops_d[k] = copy(v_buf.at[k], x_buf.at[k], 3 * chunks + k, far)
-    for k in order:
-        mine = zl if k < chunks // 2 else y
-        part = kept[k, zh, mine] + r_buf[k, zh, mine].astype(F32) + u_buf[k, zh].astype(F32)
-        ops_d[k].wait_recv()
-        part = part + x_buf[k].astype(F32)
-        wg[zh, zl, y, c, :, k * CH : (k + 1) * CH] = part[GB:, :].astype(BF16)
-        own[:, k * CH : (k + 1) * CH] = part[:GB, :]
-
-    def finish():
-        part = own[...]
-        high = part.astype(BF16)
-        low = (part - high.astype(F32)).astype(BF16)
-        total = mm(high, wkv_ref[...], 1, 1) + mm(low, wkv_ref[...], 1, 1)
-        dglob_ref[...] = total.astype(BF16)
-
-    gather_steps(wg, wg.shape[4] // 2, copy, 4 * chunks, at, to, finish)
-    for group in (ops_a, ops_b, ops_c, ops_d):
-        for k in order:
-            group[k].wait_send()
+
+    def keep_pairs(k):
+        def done(total):
+            own[:, k * CH : (k + 1) * CH] = total
+
+        return done
+
+    def keep_weights(k):
+        def done(total):
+            wg[zh, zl, y, c, :, k * feat : (k + 1) * feat] = total.astype(BF16)
+
+        return done
+
+    steps = {}
+    for k in range(2):
+        bufs = [buf.at[k] for buf in weight_bufs]
+        steps["w", k] = halve_steps(
+            k == 0, wpay_ref.at[k], bufs, copy, 4 * k, at, to, keep_weights(k)
+        )
+    for k in range(chunks):
+        bufs = [buf.at[k] for buf in pair_bufs]
+        steps["p", k] = halve_steps(
+            k < chunks // 2, pay_ref.at[k], bufs, copy, 8 + 4 * k, at, to, keep_pairs(k)
+        )
+    share = gather_steps(wg, wg.shape[4] // 2, copy, 8 + 4 * chunks, at, to)
+
+    def weights():
+        for k in range(2):
+            next(steps["w", k])
+
+    def pairs(first):
+        for k in range(first, chunks // 2, 2):
+            next(steps["p", k])
+            next(steps["p", k + chunks // 2])
+
+    weights()
+    pairs(0)
+    pairs(1)
+    weights()
+    pairs(0)
+    weights()
+    pairs(1)
+    weights()
+    pairs(0)
+    weights()
+    next(share)
+    pairs(1)
+    next(share)
+    pairs(0)
+    next(share)
+    pairs(1)
+    next(share)
+    pairs(0)
+    pairs(1)
+    part = own[...]
+    high = part.astype(BF16)
+    low = (part - high.astype(F32)).astype(BF16)
+    total = mm(high, wkv_ref[...], 1, 1) + mm(low, wkv_ref[...], 1, 1)
+    dglob_ref[...] = total.astype(BF16)
+    next(share)
+    weights()
+    pairs(0)
+    pairs(1)
 
 
 def finish_kernel(norm, dglob_in, wg_ref, dglob_ref, gq_ref, gkv_ref, go_ref):
@@ -280,17 +334,18 @@
     tokens = tokens.reshape(SUB * GB, feat)
     slots = LIST * GB
     wide = feat // HD * BT
-    depth = GB + 2 * feat // SUB
+    few = 2 * feat // SUB
     smem = [pl.BlockSpec(memory_space=pltpu.SMEM)] * 2
-    output, d_nest, payload = pl.pallas_call(
+    output, d_nest, payload, wide_payload = pl.pallas_call(
         attend_kernel,
         out_shape=(
             jax.ShapeDtypeStruct((rows, feat), BF16),
             jax.ShapeDtypeStruct((rows, feat), BF16),
-            jax.ShapeDtypeStruct((2 * feat // CH, SUB, depth, CH), BF16),
+            jax.ShapeDtypeStruct((2 * feat // CH, SUB, GB, CH), BF16),
+            jax.ShapeDtypeStruct((2, SUB, few, feat), BF16),
         ),
         in_specs=smem + vmem(6),
-        out_specs=tuple(vmem(3)),
+        out_specs=tuple(vmem(4)),
         scratch_shapes=[
             pltpu.VMEM((SUB * GB, 2 * feat), BF16),
             pltpu.VMEM((rows, feat), BF16),
@@ -308,32 +363,33 @@
         compiler_params=pltpu.CompilerParams(vmem_limit_bytes=VMEM_LIMIT),
     )(block_ids, list_length, tokens, nest_tokens, d_output, w_query, w_keyval, w_out)
     n = 2 * feat // CH
-    payload = payload.reshape(n, 2, 2, 2, 2, depth, CH)
+    payload = payload.reshape(n, 2, 2, 2, 2, GB, CH)
+    wide_payload = wide_payload.reshape(2, 2, 2, 2, 2, few, feat)
+    scratch = []
+    for count, block in ((n, (GB, CH)), (2, (few, feat))):
+        for lead, dtype in (
+            ((2, 2, 2), BF16), ((2, 2), BF16), ((2, 2), BF16), ((2, 2), F32),
+            ((2,), BF16), ((2,), BF16), ((), BF16), ((), BF16),
+        ):
+            scratch.append(pltpu.VMEM((count, *lead, *block), dtype))
+    copies = 8 + 4 * n + 6
     d_global, sums = pl.pallas_call(
         reduce_kernel,
         out_shape=(
             jax.ShapeDtypeStruct((GB, feat), BF16),
-            jax.ShapeDtypeStruct((2, 2, 2, 2, depth - GB, 2 * feat), BF16),
+            jax.ShapeDtypeStruct((2, 2, 2, 2, few, 2 * feat), BF16),
         ),
-        in_specs=vmem(2),
+        in_specs=vmem(3),
         out_specs=tuple(vmem(2)),
-        scratch_shapes=[
-            pltpu.VMEM((n, 2, 2, 2, depth, CH), BF16),
-            pltpu.VMEM((n, 2, 2, depth, CH), BF16),
-            pltpu.VMEM((n, 2, 2, depth, CH), BF16),
-            pltpu.VMEM((n, 2, 2, depth, CH), F32),
-            pltpu.VMEM((n, 2, depth, CH), BF16),
-            pltpu.VMEM((n, 2, depth, CH), BF16),
-            pltpu.VMEM((n, depth, CH), BF16),
-            pltpu.VMEM((n, depth, CH), BF16),
+        scratch_shapes=scratch + [
             pltpu.VMEM((GB, 2 * feat), F32),
-            pltpu.SemaphoreType.DMA((4 * n + 6,)),
-            pltpu.SemaphoreType.DMA((4 * n + 6,)),
+            pltpu.SemaphoreType.DMA((copies,)),
+            pltpu.SemaphoreType.DMA((copies,)),
         ],
         compiler_params=pltpu.CompilerParams(
             collective_id=1, has_side_effects=True, vmem_limit_bytes=VMEM_LIMIT
         ),
-    )(payload, w_keyval)
+    )(payload, wide_payload, w_keyval)
     d_global, grad_q, grad_kv, grad_o = pl.pallas_call(
         functools.partial(finish_kernel, norm),
         out_shape=(

time: 78.7 us -> 69.6 us (0.88)
  Pallas kernels: 77.8 us -> 68.7 us
    pallas_call x1, Pallas kernels: 37.7 us -> 29.1 us  [shards(): pl.pallas_call(reduce_kernel, out_shape=(jax.ShapeDtypeStruct((GB, feat),...]
where the time goes in v3:
time: 69.6 us; the launch traced here: 69.4 us
  Pallas kernels  68.7 us (99%)
    pallas_call x1, Pallas kernels, shards(): pl.pallas_call(reduce_kernel, out_shape=(jax.ShapeDtypeStruct((GB, feat),...  29.1 us
    pallas_call x1, Pallas kernels, shards(): pl.pallas_call(gather_kernel, out_shape=jax.ShapeDtypeStruct((2, 2, 2, 2,...  19.8 us
    pallas_call x1, Pallas kernels, shards(): pl.pallas_call(attend_kernel, out_shape=(jax.ShapeDtypeStruct((rows, feat...  17.7 us
    pallas_call x1, Pallas kernels, shards(): pl.pallas_call(functools.partial(finish_kernel, norm), out_shape=(jax.Sha...  2.12 us

profile of v3, /device:TPU:0, one launch (start us, length us, event | category | flops | bytes accessed | tf_op | source)
XLA Modules:
  0.0 69.4 jit_solution(9868428915458753345)
XLA Ops:
  0.6 19.8 %shard_map.127 = bf16[2,2,2,2,128,256]{5,4,3,2,1,0:T(8,128)(2,1)} custom-call(bf16[128,256]{1,0:T(8,128)(2,1)} %tok_ref.1), custom_call_target="tpu_custom_call" | custom-call | tf_op jit(solution)/shard_map/pallas_call | solution.py:324
  20.4 17.7 %shard_map.128 = (bf16[512,256]{1,0:T(8,128)(2,1)}, bf16[512,256]{1,0:T(8,128)(2,1)}, bf16[4,16,128,128]{3,2,1,0:T(8,128)(2,1)}, bf16[2,16,32,256]{3,2,1,0:T(8,128)(2,1)}) custom-call(s32[4,4]{1,0:T(4,128)} %ids_ref.1, s32[4]{0:T(128)} %len_ref.1, bf16[2048,256]{1,0:T(8,128)(2,1)} %bitcast.4, bf16[512,256]{1,0:T(8,128)(2,1)} %nest_ref.1, ...), custom_call_target="tpu_custom_call" | custom-call | tf_op jit(solution)/shard_map/pallas_call | solution.py:339
  38.1 29.1 %shard_map.129 = (bf16[128,256]{1,0:T(8,128)(2,1)}, bf16[2,2,2,2,32,512]{5,4,3,2,1,0:T(8,128)(2,1)}) custom-call(bf16[4,2,2,2,2,128,128]{6,5,4,3,2,1,0:T(8,128)(2,1)} %bitcast.5, bf16[2,2,2,2,2,32,256]{6,5,4,3,2,1,0:T(8,128)(2,1)} %bitcast.7, bf16[256,512]{1,0:T(8,128)(2,1)} %wkv_ref.3), custom_call_target="tpu_custom_call" | custom-call | tf_op jit(solution)/shard_map/pallas_call | solution.py:376
  67.3 2.1 %shard_map.130 = (bf16[128,256]{1,0:T(8,128)(2,1)}, f32[256,256]{1,0:T(8,128)}, f32[256,512]{1,0:T(8,128)}, f32[256,256]{1,0:T(8,128)}) custom-call(bf16[128,256]{1,0:T(8,128)(2,1)} %get-tuple-element.20.dglob_in, bf16[512,512]{1,0:T(8,128)(2,1)} %bitcast.6), custom_call_target="tpu_custom_call" | custom-call | tf_op jit(solution)/shard_map/pallas_call | solution.py:393

commit v4 on v3

--- a/solution.py
+++ b/solution.py
@@ -15,7 +15,7 @@
 SUB = 16
 F32 = jnp.float32
 BF16 = jnp.bfloat16
-VMEM_LIMIT = 56 * 1024 * 1024
+VMEM_LIMIT = 30 * 1024 * 1024
 
 
 def mm(a, b, ca=1, cb=0):
@@ -129,14 +129,52 @@
     yield
 
 
+def spread_steps(side_first, buf, rows, copy, k, at, to):
+    zh, zl, y, c = at
+    far, near, side, core = to
+
+    def go(ref, device):
+        ops.append(copy(ref, ref, k + len(ops), device))
+
+    ops = []
+    go(buf.at[zh, zl, y, c, rows], far)
+    yield
+    ops[0].wait_recv()
+    go(buf.at[:, zl, y, c, rows], side if side_first else near)
+    yield
+    ops[1].wait_recv()
+    if side_first:
+        go(buf.at[:, zl, :, c, rows], near)
+    else:
+        go(buf.at[:, :, y, c, rows], side)
+    yield
+    ops[2].wait_recv()
+    go(buf.at[:, :, :, c, rows], core)
+    yield
+    ops[3].wait_recv()
+    for op in ops:
+        op.wait_send()
+    yield
+
+
+PIECES = 4
+
+
 def gather_kernel(tok_ref, all_ref, send, recv):
     base, *at = coords()
     to = partners(base, *at)
     zh, zl, y, c = at
     all_ref[zh, zl, y, c] = tok_ref[...]
     greet(to)
-    for _ in gather_steps(all_ref, tok_ref.shape[0] // 2, sender(send, recv), 0, at, to):
-        pass
+    copy = sender(send, recv)
+    size = tok_ref.shape[0] // PIECES
+    steps = [
+        spread_steps(k % 2 == 0, all_ref, pl.ds(k * size, size), copy, 4 * k, at, to)
+        for k in range(PIECES)
+    ]
+    for _ in range(5):
+        for step in steps:
+            next(step)
 
 
 def attend_kernel(
@@ -326,7 +364,7 @@
         out_shape=jax.ShapeDtypeStruct((2, 2, 2, 2, GB, feat), BF16),
         in_specs=vmem(1),
         out_specs=vmem(1)[0],
-        scratch_shapes=[pltpu.SemaphoreType.DMA((6,)), pltpu.SemaphoreType.DMA((6,))],
+        scratch_shapes=[pltpu.SemaphoreType.DMA((4 * PIECES,))] * 2,
         compiler_params=pltpu.CompilerParams(
             collective_id=0, has_side_effects=True, vmem_limit_bytes=VMEM_LIMIT
         ),

time: 69.6 us -> 69.1 us (level)
  Pallas kernels: 68.7 us -> 61.3 us
  local copies, waits for them, and re-layouts: 0 us -> 6.82 us
    unnamed x0 -> x16, local copies, waits for them, and re-layouts: none -> 6.82 us
    pallas_call x1, Pallas kernels: 19.8 us -> 16.6 us  [shards(): pl.pallas_call(gather_kernel, out_shape=jax.ShapeDtypeStruct((2, 2, 2, 2,...]
    pallas_call x1, Pallas kernels: 17.7 us -> 16 us  [shards(): pl.pallas_call(attend_kernel, out_shape=(jax.ShapeDtypeStruct((rows, feat...]
    pallas_call x1, Pallas kernels: 29.1 us -> 27.6 us  [shards(): pl.pallas_call(reduce_kernel, out_shape=(jax.ShapeDtypeStruct((GB, feat),...]
    pallas_call x1, Pallas kernels: 2.12 us -> 1.04 us  [shards(): pl.pallas_call(functools.partial(finish_kernel, norm), out_shape=(jax.Sha...]
where the time goes in v4:
time: 69.1 us; the launch traced here: 68.8 us
  Pallas kernels  61.3 us (89%)
  local copies, waits for them, and re-layouts  6.82 us (10%)
    pallas_call x1, Pallas kernels, shards(): pl.pallas_call(reduce_kernel, out_shape=(jax.ShapeDtypeStruct((GB, feat),...  27.6 us
    pallas_call x1, Pallas kernels, shards(): pl.pallas_call(gather_kernel, out_shape=jax.ShapeDtypeStruct((2, 2, 2, 2,...  16.6 us
    pallas_call x1, Pallas kernels, shards(): pl.pallas_call(attend_kernel, out_shape=(jax.ShapeDtypeStruct((rows, feat...  16 us
    unnamed x16, local copies, waits for them, and re-layouts  6.82 us

profile of v4, /device:TPU:0, one launch (start us, length us, event | category | flops | bytes accessed | tf_op | source)
XLA Modules:
  0.0 68.8 jit_solution(15814481157892826642)
XLA Ops:
  0.6 0.0 copy-start.5
  0.6 0.8 %copy-done.5 = bf16[128,256]{1,0:T(8,128)(2,1)S(1)} copy-done((bf16[128,256]{1,0:T(8,128)(2,1)S(1)}, bf16[128,256]{1,0:T(8,128)(2,1)}, u32[]{:S(2)}) %copy-start.5) | copy-done | bytes 65560
  1.5 16.6 %shard_map.127 = bf16[2,2,2,2,128,256]{5,4,3,2,1,0:T(8,128)(2,1)S(1)} custom-call(bf16[128,256]{1,0:T(8,128)(2,1)S(1)} %copy-done.5), custom_call_target="tpu_custom_call" | custom-call | tf_op jit(solution)/shard_map/pallas_call | solution.py:362
  18.1 0.0 copy-start
  18.1 0.9 %copy-done = bf16[256,512]{1,0:T(8,128)(2,1)S(1)} copy-done((bf16[256,512]{1,0:T(8,128)(2,1)S(1)}, bf16[256,512]{1,0:T(8,128)(2,1)}, u32[]{:S(2)}) %copy-start) | copy-done | bytes 262168
  19.1 0.0 copy-start.1
  19.1 0.9 %copy-done.1 = bf16[512,256]{1,0:T(8,128)(2,1)S(1)} copy-done((bf16[512,256]{1,0:T(8,128)(2,1)S(1)}, bf16[512,256]{1,0:T(8,128)(2,1)}, u32[]{:S(2)}) %copy-start.1) | copy-done | bytes 262168
  20.0 0.0 copy-start.2
  20.0 0.9 %copy-done.2 = bf16[512,256]{1,0:T(8,128)(2,1)S(1)} copy-done((bf16[512,256]{1,0:T(8,128)(2,1)S(1)}, bf16[512,256]{1,0:T(8,128)(2,1)}, u32[]{:S(2)}) %copy-start.2) | copy-done | bytes 262168
  21.0 0.0 copy-start.3
  21.0 0.9 %copy-done.3 = bf16[256,256]{1,0:T(8,128)(2,1)S(1)} copy-done((bf16[256,256]{1,0:T(8,128)(2,1)S(1)}, bf16[256,256]{1,0:T(8,128)(2,1)}, u32[]{:S(2)}) %copy-start.3) | copy-done | bytes 131096
  21.9 0.0 copy-start.4
  21.9 0.9 %copy-done.4 = bf16[256,256]{1,0:T(8,128)(2,1)S(1)} copy-done((bf16[256,256]{1,0:T(8,128)(2,1)S(1)}, bf16[256,256]{1,0:T(8,128)(2,1)}, u32[]{:S(2)}) %copy-start.4) | copy-done | bytes 131096
  22.8 0.0 copy-start.6
  22.8 0.7 copy-done.6
  23.5 0.0 copy-start.7
  23.5 0.7 copy-done.7
  24.1 16.0 %shard_map.128 = (bf16[512,256]{1,0:T(8,128)(2,1)}, bf16[512,256]{1,0:T(8,128)(2,1)}, bf16[4,16,128,128]{3,2,1,0:T(8,128)(2,1)S(1)}, bf16[2,16,32,256]{3,2,1,0:T(8,128)(2,1)S(1)}) custom-call(s32[4,4]{1,0:T(4,128)S(1)} %copy-done.6, s32[4]{0:T(128)S(1)} %copy-done.7, bf16[2048,256]{1,0:T(8,128)(2,1)S(1)} %bitcast.4, bf16[512,256]{1,0:T(8,128)(2,1)S(1)} %copy-done.1, ...), custom_call_target="tpu_custom_call" | custom-call | tf_op jit(solution)/shard_map/pallas_call | solution.py:377
  40.1 27.6 %shard_map.129 = (bf16[128,256]{1,0:T(8,128)(2,1)S(1)}, bf16[2,2,2,2,32,512]{5,4,3,2,1,0:T(8,128)(2,1)S(1)}) custom-call(bf16[4,2,2,2,2,128,128]{6,5,4,3,2,1,0:T(8,128)(2,1)S(1)} %bitcast.5, bf16[2,2,2,2,2,32,256]{6,5,4,3,2,1,0:T(8,128)(2,1)S(1)} %bitcast.7, bf16[256,512]{1,0:T(8,128)(2,1)S(1)} %copy-done), custom_call_target="tpu_custom_call" | custom-call | tf_op jit(solution)/shard_map/pallas_call | solution.py:414
  67.7 1.0 %shard_map.130 = (bf16[128,256]{1,0:T(8,128)(2,1)}, f32[256,256]{1,0:T(8,128)}, f32[256,512]{1,0:T(8,128)}, f32[256,256]{1,0:T(8,128)}) custom-call(bf16[128,256]{1,0:T(8,128)(2,1)S(1)} %get-tuple-element.20.dglob_in, bf16[512,512]{1,0:T(8,128)(2,1)S(1)} %bitcast.6), custom_call_target="tpu_custom_call" | custom-call | tf_op jit(solution)/shard_map/pallas_call | solution.py:431
Async XLA Ops:
  0.6 0.8 %copy-start.5 = (bf16[128,256]{1,0:T(8,128)(2,1)S(1)}, bf16[128,256]{1,0:T(8,128)(2,1)}, u32[]{:S(2)}) copy-start(bf16[128,256]{1,0:T(8,128)(2,1)} %tok_ref.1) | copy-start | bytes 196612
  18.1 1.0 %copy-start = (bf16[256,512]{1,0:T(8,128)(2,1)S(1)}, bf16[256,512]{1,0:T(8,128)(2,1)}, u32[]{:S(2)}) copy-start(bf16[256,512]{1,0:T(8,128)(2,1)} %wkv_ref.3) | copy-start | bytes 786436
  19.1 0.9 %copy-start.1 = (bf16[512,256]{1,0:T(8,128)(2,1)S(1)}, bf16[512,256]{1,0:T(8,128)(2,1)}, u32[]{:S(2)}) copy-start(bf16[512,256]{1,0:T(8,128)(2,1)} %nest_ref.1) | copy-start | bytes 786436
  20.0 0.9 %copy-start.2 = (bf16[512,256]{1,0:T(8,128)(2,1)S(1)}, bf16[512,256]{1,0:T(8,128)(2,1)}, u32[]{:S(2)}) copy-start(bf16[512,256]{1,0:T(8,128)(2,1)} %dout_ref.1) | copy-start | bytes 786436
  21.0 0.9 %copy-start.3 = (bf16[256,256]{1,0:T(8,128)(2,1)S(1)}, bf16[256,256]{1,0:T(8,128)(2,1)}, u32[]{:S(2)}) copy-start(bf16[256,256]{1,0:T(8,128)(2,1)} %wq_ref.1) | copy-start | bytes 393220
  21.9 0.9 %copy-start.4 = (bf16[256,256]{1,0:T(8,128)(2,1)S(1)}, bf16[256,256]{1,0:T(8,128)(2,1)}, u32[]{:S(2)}) copy-start(bf16[256,256]{1,0:T(8,128)(2,1)} %wo_ref.1) | copy-start | bytes 393220
  22.8 0.7 copy-start.6
  23.5 0.7 copy-start.7

commit v5 on v4

--- a/solution.py
+++ b/solution.py
@@ -15,7 +15,7 @@
 SUB = 16
 F32 = jnp.float32
 BF16 = jnp.bfloat16
-VMEM_LIMIT = 30 * 1024 * 1024
+VMEM_LIMIT = 56 * 1024 * 1024
 
 
 def mm(a, b, ca=1, cb=0):

time: 69.1 us -> 69.4 us (level)
  Pallas kernels: 61.3 us -> 68.5 us
  local copies, waits for them, and re-layouts: 6.82 us -> 0 us
    unnamed x16 -> x0, local copies, waits for them, and re-layouts: 6.82 us -> none
    pallas_call x1, Pallas kernels: 27.6 us -> 30.2 us  [shards(): pl.pallas_call(reduce_kernel, out_shape=(jax.ShapeDtypeStruct((GB, feat),...]
    pallas_call x1, Pallas kernels: 16.6 us -> 18.5 us  [shards(): pl.pallas_call(gather_kernel, out_shape=jax.ShapeDtypeStruct((2, 2, 2, 2,...]
    pallas_call x1, Pallas kernels: 16 us -> 17.6 us  [shards(): pl.pallas_call(attend_kernel, out_shape=(jax.ShapeDtypeStruct((rows, feat...]
    pallas_call x1, Pallas kernels: 1.04 us -> 2.12 us  [shards(): pl.pallas_call(functools.partial(finish_kernel, norm), out_shape=(jax.Sha...]
where the time goes in v5:
time: 69.4 us; the launch traced here: 69.1 us
  Pallas kernels  68.5 us (99%)
    pallas_call x1, Pallas kernels, shards(): pl.pallas_call(reduce_kernel, out_shape=(jax.ShapeDtypeStruct((GB, feat),...  30.2 us
    pallas_call x1, Pallas kernels, shards(): pl.pallas_call(gather_kernel, out_shape=jax.ShapeDtypeStruct((2, 2, 2, 2,...  18.5 us
    pallas_call x1, Pallas kernels, shards(): pl.pallas_call(attend_kernel, out_shape=(jax.ShapeDtypeStruct((rows, feat...  17.6 us
    pallas_call x1, Pallas kernels, shards(): pl.pallas_call(functools.partial(finish_kernel, norm), out_shape=(jax.Sha...  2.12 us

profile of v5, /device:TPU:0, one launch (start us, length us, event | category | flops | bytes accessed | tf_op | source)
XLA Modules:
  0.0 69.1 jit_solution(17510630991925873751)
XLA Ops:
  0.6 18.5 %shard_map.127 = bf16[2,2,2,2,128,256]{5,4,3,2,1,0:T(8,128)(2,1)} custom-call(bf16[128,256]{1,0:T(8,128)(2,1)} %tok_ref.1), custom_call_target="tpu_custom_call" | custom-call | tf_op jit(solution)/shard_map/pallas_call | solution.py:362
  19.1 17.6 %shard_map.128 = (bf16[512,256]{1,0:T(8,128)(2,1)}, bf16[512,256]{1,0:T(8,128)(2,1)}, bf16[4,16,128,128]{3,2,1,0:T(8,128)(2,1)}, bf16[2,16,32,256]{3,2,1,0:T(8,128)(2,1)}) custom-call(s32[4,4]{1,0:T(4,128)} %ids_ref.1, s32[4]{0:T(128)} %len_ref.1, bf16[2048,256]{1,0:T(8,128)(2,1)} %bitcast.4, bf16[512,256]{1,0:T(8,128)(2,1)} %nest_ref.1, ...), custom_call_target="tpu_custom_call" | custom-call | tf_op jit(solution)/shard_map/pallas_call | solution.py:377
  36.8 30.2 %shard_map.129 = (bf16[128,256]{1,0:T(8,128)(2,1)}, bf16[2,2,2,2,32,512]{5,4,3,2,1,0:T(8,128)(2,1)}) custom-call(bf16[4,2,2,2,2,128,128]{6,5,4,3,2,1,0:T(8,128)(2,1)} %bitcast.5, bf16[2,2,2,2,2,32,256]{6,5,4,3,2,1,0:T(8,128)(2,1)} %bitcast.7, bf16[256,512]{1,0:T(8,128)(2,1)} %wkv_ref.3), custom_call_target="tpu_custom_call" | custom-call | tf_op jit(solution)/shard_map/pallas_call | solution.py:414
  67.0 2.1 %shard_map.130 = (bf16[128,256]{1,0:T(8,128)(2,1)}, f32[256,256]{1,0:T(8,128)}, f32[256,512]{1,0:T(8,128)}, f32[256,256]{1,0:T(8,128)}) custom-call(bf16[128,256]{1,0:T(8,128)(2,1)} %get-tuple-element.20.dglob_in, bf16[512,512]{1,0:T(8,128)(2,1)} %bitcast.6), custom_call_target="tpu_custom_call" | custom-call | tf_op jit(solution)/shard_map/pallas_call | solution.py:431
